TPU v7x, 128 devices: a whole 4x4x4 slice. The times are simulated.
128 devices in a mesh: group: 4 (over z), depth: 8 (over x, core), image: 4 (over y).
Axes of the slice: x: 4, y: 4, z: 4, core: 2. Of those that a mesh axis runs over, the one named last changes fastest.
Arguments:
- density: float32 [64, 192, 512], P('depth', 'group', 'image'), may hold values from 0.5 to 1.5
- velocity: float32 [3, 64, 192, 512], P(None, 'depth', 'group', 'image'), may hold values from -1.2 to 1.2
- pressure: float32 [64, 192, 512], P('depth', 'group', 'image'), may hold values from 0.5 to 1.5
- palette: float32 [4, 256], replicated, may hold values from 0.2 to 2
- palette_index: int32 [8, 256], replicated, may hold values from 0 to 255
Outputs:
- fluid_state: float32 [5, 64, 192, 512], P(None, 'depth', 'group', 'image')
- picture: float32 [8, 3, 192, 512], P('depth', None, 'group', 'image')
All inputs are finite; a program needn't handle non-finite values.
Results may differ from a plain program's by a relative error of at most 0.0003.
Values sent between devices are 32-bit elements; how exact they have to be, the bound alone decides.
A program may use at most 128 MiB of HBM per device.

v0:
```python
import jax
import jax.numpy as jnp
from jax import lax
from jax.sharding import PartitionSpec as P

HEAT_RATIO = 1.4
COURANT = 0.8


def extended(array, sides, width, wrap):
    for axis, dim in sides:
        size, length = (lax.axis_size(axis), array.shape[dim])
        up = [(i, (i + 1) % size) for i in range(size if wrap else size - 1)]
        down = [(j, i) for i, j in up]
        last = lax.slice_in_dim(array, length - width, length, axis=dim)
        first = lax.slice_in_dim(array, 0, width, axis=dim)
        before = lax.ppermute(last, axis, up)
        after = lax.ppermute(first, axis, down)
        array = jnp.concatenate([before, array, after], axis=dim)
    return array


def passed_along(block, axis, distance):
    devices = range(lax.axis_size(axis))
    route = [(i - distance, i) for i in devices if i - distance in devices]
    return lax.ppermute(block, axis, route)


def entering(array, axis, combine, identity):
    size, here = (lax.axis_size(axis), lax.axis_index(axis))
    everything = lax.all_gather(array, axis)
    start = jnp.broadcast_to(jnp.asarray(identity, array.dtype), array.shape)

    def lap(k, before):
        reached = k < here
        new = combine(before, everything[k])
        return jnp.where(reached, new, before)

    return lax.fori_loop(0, size, lap, start)


def leading(values, direction):
    return lax.slice_in_dim(values, 0, values.shape[direction] - 1, axis=direction)


def trailing(values, direction):
    return lax.slice_in_dim(values, 1, values.shape[direction], axis=direction)


def conserved(density, velocity, pressure):
    momentum = density[None] * velocity
    kinetic = 0.5 * density * jnp.sum(velocity * velocity, axis=0)
    return jnp.concatenate(
        [density[None], momentum, (pressure / (HEAT_RATIO - 1.0) + kinetic)[None]], axis=0
    )


def primitives(fluid_state):
    density = fluid_state[0]
    velocities = fluid_state[1:4] / density[None]
    kinetic = 0.5 * jnp.sum(fluid_state[1:4] * velocities, axis=0)
    pressures = (HEAT_RATIO - 1.0) * (fluid_state[4] - kinetic)
    return (density, velocities, pressures)


def euler_flux(fluid_state, component):
    density, velocities, pressures = primitives(fluid_state)
    normal = velocities[component - 1]
    rows = [
        fluid_state[0] * normal,
        fluid_state[1] * normal,
        fluid_state[2] * normal,
        fluid_state[3] * normal,
        (fluid_state[4] + pressures) * normal,
    ]
    rows[component] = rows[component] + pressures
    signal = jnp.abs(normal) + jnp.sqrt(HEAT_RATIO * pressures / density)
    return (jnp.stack(rows), signal)


def tendency(padded):
    summed = None
    for direction, component in ((1, 3), (2, 1), (3, 2)):
        strip_cells = padded
        for across in (1, 2, 3):
            if across != direction:
                strip_cells = lax.slice_in_dim(
                    strip_cells, 1, strip_cells.shape[across] - 1, axis=across
                )
        fluxes, signal = euler_flux(strip_cells, component)
        fastest_face = jnp.maximum(leading(signal, direction - 1), trailing(signal, direction - 1))
        face_flux = 0.5 * (
            leading(fluxes, direction) + trailing(fluxes, direction)
        ) - 0.5 * fastest_face[None] * (
            trailing(strip_cells, direction) - leading(strip_cells, direction)
        )
        change = trailing(face_flux, direction) - leading(face_flux, direction)
        summed = change if summed is None else summed + change
    return -summed


def wave_bound(fluid_state):
    density, velocities, pressures = primitives(fluid_state)
    return jnp.max(
        jnp.sum(jnp.abs(velocities), axis=0) + 3.0 * jnp.sqrt(HEAT_RATIO * pressures / density)
    )


def mirror_sign():
    return jnp.array([1.0, -1.0, 1.0, 1.0, 1.0], jnp.float32)[:, None, None, None]


def colour_table(palette, palette_index):
    count_tf = palette_index.shape[0]
    count_bins = palette_index.shape[1]
    onehot = (
        jnp.arange(palette.shape[1], dtype=jnp.int32)[:, None] == palette_index.reshape(-1)[None, :]
    ).astype(jnp.float32)
    table = jnp.dot(palette, onehot, precision=lax.Precision.HIGHEST)
    return (
        table.reshape(4, count_tf, count_bins).transpose(1, 0, 2).reshape(count_tf * 4, count_bins)
    )


def sheet_shares(
    screen_shades, unrolled_mass_per_volume, thermal_grid_quantity, ray_increment_distance
):
    count_bins = screen_shades.shape[1]
    position = jnp.clip(unrolled_mass_per_volume - 0.5, 0.0, 1.0) * (count_bins - 1)
    hat_weights = jnp.maximum(
        0.0, 1.0 - jnp.abs(position[None, :] - jnp.arange(count_bins, dtype=jnp.float32)[:, None])
    )
    shade_mapping_index = jnp.dot(
        screen_shades, hat_weights, precision=lax.Precision.HIGHEST
    ).reshape(screen_shades.shape[0] // 4, 4, unrolled_mass_per_volume.shape[0])
    extinct = shade_mapping_index[:, 3] * unrolled_mass_per_volume[None] * ray_increment_distance
    absorbance_entries = 1.0 - jnp.exp(-extinct)
    radiance_source = (
        shade_mapping_index[:, :3] * (absorbance_entries * thermal_grid_quantity[None])[:, None]
    )
    return (extinct, radiance_source)


def march_slab(screen_shades, density_field, heat_field, ray_increment_distance):
    count_tf = screen_shades.shape[0] // 4
    planes = density_field.shape[0]
    cell_count = density_field.shape[1] * density_field.shape[2]

    def march_plane(carried, slab):
        optical, colour = carried
        extinct, radiance_source = sheet_shares(
            screen_shades, slab[0], slab[1], ray_increment_distance
        )
        return ((optical + extinct, colour + jnp.exp(-optical)[:, None] * radiance_source), None)

    initial = (
        jnp.zeros((count_tf, cell_count), jnp.float32),
        jnp.zeros((count_tf, 3, cell_count), jnp.float32),
    )
    (optical, colour), unused = lax.scan(
        march_plane,
        initial,
        (density_field.reshape(planes, cell_count), heat_field.reshape(planes, cell_count)),
    )
    return (optical, colour)


def widen(values, row_index, fluid_rows):
    sided = extended(values, (("group", 2),), 1, False)
    lower = jnp.where(row_index == 0, values[:, :, :1] * mirror_sign(), sided[:, :, :1])
    upper = jnp.where(
        row_index == fluid_rows - 1, values[:, :, -1:] * mirror_sign(), sided[:, :, -1:]
    )
    walled = jnp.concatenate([lower, values, upper], axis=2)
    return extended(walled, (("depth", 1), ("image", 3)), 1, True)


def add_terms(earlier, later):
    return earlier + later


def shards(density, velocity, pressure, palette, palette_index):
    group_count = lax.axis_size("group")
    fluid_rows = group_count - 1
    depth_count = lax.axis_size("depth")
    row_index = lax.axis_index("group")
    is_fluid = row_index < fluid_rows
    is_render = row_index == fluid_rows
    shard_state = conserved(density, velocity, pressure)
    fastest = lax.pmax(wave_bound(shard_state), ("group", "depth", "image"))
    time_step = COURANT / fastest
    shard_rows = shard_state.shape[2]
    brick_rows = shard_rows * group_count // fluid_rows
    step_rows = brick_rows - shard_rows
    following = passed_along(shard_state, "group", -1)
    joined = jnp.concatenate([shard_state, following], axis=2)
    initial_state = lax.dynamic_slice_in_dim(joined, row_index * step_rows, brick_rows, axis=2)

    def change(values):
        padded = widen(values, row_index, fluid_rows)
        return lax.cond(is_fluid, tendency, lambda unused: jnp.zeros_like(values), padded)

    section_one = initial_state + time_step * change(initial_state)
    section_two = 0.75 * initial_state + 0.25 * (section_one + time_step * change(section_one))
    section_three = initial_state / 3.0 + 2.0 / 3.0 * (
        section_two + time_step * change(section_two)
    )
    previous = passed_along(section_three, "group", 1)
    joined_out = jnp.concatenate([previous, section_three], axis=2)
    fluid_state = lax.dynamic_slice_in_dim(
        joined_out, brick_rows - row_index * step_rows, shard_rows, axis=2
    )
    field_density, velocities, pressures = primitives(section_three)
    safe_density = jnp.where(is_fluid, field_density, 1.0)
    safe_heat = jnp.where(is_fluid, pressures / field_density, 1.0)
    ray_increment_distance = 2.0 / (section_three.shape[1] * depth_count)
    screen_shades = colour_table(palette, palette_index)
    count_tf = palette_index.shape[0]
    width_y = section_three.shape[3]
    picture_rows = fluid_rows * brick_rows
    all_density, all_heat = (
        lax.all_gather(safe_density, "group", axis=1, tiled=True),
        lax.all_gather(safe_heat, "group", axis=1, tiled=True),
    )
    block_density = all_density[:, :picture_rows]
    block_heat = all_heat[:, :picture_rows]
    rows_here = block_density.shape[1]

    def render():
        optical, colour = march_slab(
            screen_shades, block_density, block_heat, ray_increment_distance
        )
        return (
            optical.reshape(count_tf, rows_here, width_y),
            colour.reshape(count_tf, 3, rows_here, width_y),
        )

    def skip():
        return (
            jnp.zeros((count_tf, rows_here, width_y), jnp.float32),
            jnp.zeros((count_tf, 3, rows_here, width_y), jnp.float32),
        )

    optical, colour = lax.cond(is_render, render, skip)
    per_dev = count_tf // depth_count
    before = entering(optical, "depth", add_terms, jnp.zeros_like(optical))
    weighted = jnp.exp(-before)[:, None] * colour
    arranged = (
        weighted.reshape(depth_count, per_dev, 3, group_count, shard_rows, width_y)
        .transpose(3, 0, 1, 2, 4, 5)
        .reshape(group_count * depth_count * per_dev, 3, shard_rows, width_y)
    )
    picture = lax.psum_scatter(arranged, ("group", "depth"), scatter_dimension=0, tiled=True)
    return (fluid_state, picture)


def solution(mesh):
    return jax.shard_map(
        shards,
        mesh=mesh,
        in_specs=(
            P("depth", "group", "image"),
            P(None, "depth", "group", "image"),
            P("depth", "group", "image"),
            P(),
            P(),
        ),
        out_specs=(P(None, "depth", "group", "image"), P("depth", None, "group", "image")),
        check_vma=False,
    )
```

profile of v0, /device:TPU:1, one launch (start us, length us, event | category | flops | bytes accessed | tf_op | source)
XLA Modules:
  0.0 926.6 jit_solution(12459266574822261989)
XLA Ops:
  7.2 1.5 multiply_reduce_fusion.9
  11.0 24.5 %collective-permute-done = f32[5,8,48,128]{3,2,1,0:T(8,128)S(1)} collective-permute-done((f32[5,8,48,128]{3,2,1,0:T(8,128)S(1)}, f32[5,8,48,128]{3,2,1,0:T(8,128)S(1)}, u32[]{:S(2)}, u32[]{:S(2)}) %collective-permute-start) | collective-permute-done | bytes 983072 | tf_op jit(solution)/shard_map/ppermute | solution.py:26
  35.7 3.4 collective-permute-start.1
  40.5 3.2 collective-permute-done.2
  43.9 2.8 collective-permute-start.4
  47.8 3.5 collective-permute-done.4
  51.5 1.8 fusion.109
  53.4 3.1 copy.136
  56.5 2.7 collective-permute-start.6
  59.2 1.6 copy.135
  60.8 65.2 %pmax.7 = f32[]{:T(128)} all-reduce(f32[]{:T(128)} %get-tuple-element.310), channel_id=1, replica_groups=mesh['group'=4,'depth'=8,'image'=4] {'group','depth','image'}, use_global_device_ids=true, to_apply=%region_4.0 | all-reduce | flops 1 | bytes 8 | tf_op jit(solution)/shard_map/pmax | solution.py:190
  126.7 1.5 copy.111
  128.2 2.7 copy.110
  131.0 6.3 pad_maximum_fusion
  137.2 12.3 %conditional.4 = (f32[5,8,64,128]{3,2,1,0:T(8,128)S(1)}) conditional(s32[]{:T(128)} %convert_element_type.4, () %tuple.60, f32[5,10,66,130]{3,2,1,0:T(8,128)} %pad_maximum_fusion), branch_computations={%region_5.6_spmd, %region_6.10_spmd} | conditional | flops 13370877 | bytes 73016488 | solution.py:201
  138.5 2.1 multiply_reduce_fusion
  142.2 1.5 fusion.1
  150.7 1.6 multiply_add_fusion.2
  152.3 2.9 collective-permute-start.7
  156.5 3.2 collective-permute-done.8
  159.9 2.3 collective-permute-start.10
  162.2 2.8 collective-permute-done.10
  165.2 2.4 fusion.108
  167.6 2.5 copy.138
  170.1 2.1 collective-permute-start.12
  172.2 2.5 copy.137
  175.1 2.0 copy.119
  177.1 2.1 collective-permute-done.11
  179.1 1.9 copy.118
  181.1 6.5 pad_maximum_fusion.1
  187.6 12.1 %conditional.5 = (f32[5,8,64,128]{3,2,1,0:T(8,128)S(1)}) conditional(s32[]{:T(128)} %convert_element_type.4, () %tuple.61, f32[5,10,66,130]{3,2,1,0:T(8,128)} %pad_maximum_fusion.1), branch_computations={%region_10.11_spmd, %region_11.15_spmd} | conditional | flops 13370877 | bytes 73016488 | solution.py:201
  188.7 2.1 multiply_reduce_fusion.3
  192.3 1.5 fusion.28
  200.7 2.2 multiply_add_fusion.1
  203.0 1.6 collective-permute-start.13
  204.5 1.5 collective-permute-start.14
  206.0 3.0 collective-permute-done.14
  209.2 6.0 collective-permute-start.16
  215.2 2.0 collective-permute-done.16
  217.9 2.4 fusion.107
  220.3 2.5 copy.140
  222.8 2.5 copy.139
  225.3 1.5 collective-permute-start.17
  226.8 2.0 copy.127
  229.4 1.9 copy.126
  231.3 6.5 pad_maximum_fusion.2
  237.8 13.1 %conditional.6 = (f32[5,8,64,128]{3,2,1,0:T(8,128)}) conditional(s32[]{:T(128)} %convert_element_type.4, () %tuple.62, f32[5,10,66,130]{3,2,1,0:T(8,128)} %pad_maximum_fusion.2), branch_computations={%region_15.16_spmd, %region_16.20_spmd} | conditional | flops 13370877 | bytes 73016488 | solution.py:201
  238.9 2.1 multiply_reduce_fusion.6
  242.5 1.5 fusion.55
  249.2 1.8 fusion.61
  250.9 1.8 multiply_add_fusion
  256.5 20.0 %all-gather.5.cloned.1.call-done = f32[8,256,128]{2,0,1:T(8,128)} async-done(((f32[8,64,128]{2,0,1:T(8,128)}), f32[8,256,128]{2,0,1:T(8,128)}) %all-gather.5.cloned.1.call-update) | async-done | bytes 1048592 | tf_op jit(solution)/shard_map/all_gather | solution.py:222
  276.5 26.3 %all-gather.7.cloned.1.call-done = f32[8,256,128]{2,0,1:T(8,128)} async-done(((f32[8,64,128]{2,0,1:T(8,128)}), f32[8,256,128]{2,0,1:T(8,128)}) %all-gather.7.cloned.1.call-update) | async-done | bytes 1048592 | tf_op jit(solution)/shard_map/all_gather | solution.py:223
  302.7 2.8 conditional.7
  303.7 1.6 broadcast.355
  305.6 511.5 %all-gather.9.cloned.1.call-done = f32[64,192,128]{2,0,1:T(8,128)} async-done(((f32[8,192,128]{2,0,1:T(8,128)}), f32[64,192,128]{2,0,1:T(8,128)}) %all-gather.9.cloned.1.call-update) | async-done | bytes 6291472 | tf_op jit(solution)/shard_map/all_gather | solution.py:31
  817.1 9.0 copy.131
  826.1 11.4 %while.29 = (s32[]{:T(128)}, f32[8,192,128]{2,1,0:T(8,128)S(1)}, s32[]{:T(128)}, f32[8,8,192,128]{3,2,1,0:T(8,128)}, s32[]{:T(128)}, /*index=5*/s32[]{:T(128)}) while((s32[]{:T(128)}, f32[8,192,128]{2,1,0:T(8,128)S(1)}, s32[]{:T(128)}, f32[8,8,192,128]{3,2,1,0:T(8,128)}, s32[]{:T(128)}, /*index=5*/s32[]{:T(128)}) %tuple.151), condition=%wide.region_26.27_spmd.clone, body=%wide.region_25.26_spmd.clone.sunk | while | flops 589828 | bytes 2359397 | solution.py:39
  834.7 1.4 add_select_fusion.2
  837.7 2.0 broadcast_multiply_fusion
  839.7 1.6 copy.132
  842.6 3.4 collective-permute-start.19
  846.0 27.8 %collective-permute-done.19 = f32[5,8,64,128]{3,2,1,0:T(8,128)S(1)} collective-permute-done((f32[5,8,64,128]{3,2,1,0:T(8,128)S(1)}, f32[5,8,64,128]{3,2,1,0:T(8,128)S(1)}, u32[]{:S(2)}, u32[]{:S(2)}) %collective-permute-start.19) | collective-permute-done | bytes 1310752 | tf_op jit(solution)/shard_map/ppermute | solution.py:26
  875.0 44.8 %reduce-scatter.2.cloned.1.call-done = f32[1,3,48,128]{3,2,1,0:T(8,128)} async-done(((f32[32,3,48,128]{3,2,1,0:T(8,128)}), f32[1,3,48,128]{3,2,1,0:T(8,128)}) %reduce-scatter.2.cloned.1.call-update) | async-done | bytes 73744 | tf_op jit(solution)/shard_map/reduce_scatter | solution.py:253
  (175 shorter events, 52.5 us)
Async XLA Ops:
  7.2 248.6 %copy-start = (f32[4,256]{1,0:T(4,128)S(1)}, f32[4,256]{1,0:T(4,128)}, u32[]{:S(2)}) copy-start(f32[4,256]{1,0:T(4,128)} %param.26) | copy-start | bytes 12292
  7.2 1.6 copy-start.11
  7.2 1.6 copy-start.13
  7.2 269.3 %all-gather.5.cloned.1.call-start = ((), (), s32[]{:S(2)}) async-start(), calls=%async_computation.1 | async-start | bytes 1310720 | tf_op jit(solution)/shard_map/all_gather | solution.py:222
  9.7 34.1 %copy-start.15 = (f32[5]{0:T(128)S(1)}, f32[5]{0:T(128)}, u32[]{:S(2)}) copy-start(f32[5]{0:T(128)} %constant.209.clone) | copy-start | bytes 64
  9.7 25.8 %collective-permute-start = (f32[5,8,48,128]{3,2,1,0:T(8,128)S(1)}, f32[5,8,48,128]{3,2,1,0:T(8,128)S(1)}, u32[]{:S(2)}, u32[]{:S(2)}) collective-permute-start(f32[5,8,48,128]{3,2,1,0:T(8,128)S(1)} %pad_maximum_fusion.6), channel_id=1, source_target_pairs={{32,0},{64,32},{96,64},{33,1},{65,33},{97,65},{34,2},{66,34},{98,6... | collective-permute-start | bytes 2949128 | tf_op jit(solution)/shard_map/ppermute | solution.py:26
  35.7 4.8 collective-permute-start.1
  39.2 4.5 collective-permute-start.2
  43.8 7.5 copy-start.12
  43.9 7.4 collective-permute-start.4
  46.7 4.6 collective-permute-start.3
  56.5 70.2 %collective-permute-start.6 = (f32[5,10,66,1]{2,1,3,0:T(8,128)}, f32[5,10,66,1]{2,1,3,0:T(8,128)}, u32[]{:S(2)}, u32[]{:S(2)}) collective-permute-start(f32[5,10,66,1]{2,1,3,0:T(8,128)} %copy.136), channel_id=1, source_target_pairs={{1,0},{2,1},{3,2},{0,3},{5,4},{6,5},{7,6},{4,7},{9,8},{10,9},{11,1... | collective-permute-start | bytes 39608 | tf_op jit(solution)/shard_map/ppermute | solution.py:18
  60.8 67.4 %collective-permute-start.5 = (f32[5,10,66,1]{2,1,3,0:T(8,128)}, f32[5,10,66,1]{2,1,3,0:T(8,128)}, u32[]{:S(2)}, u32[]{:S(2)}) collective-permute-start(f32[5,10,66,1]{2,1,3,0:T(8,128)} %copy.135), channel_id=1, source_target_pairs={{0,1},{1,2},{2,3},{3,0},{4,5},{5,6},{6,7},{7,4},{8,9},{9,10},{10,1... | collective-permute-start | bytes 39608 | tf_op jit(solution)/shard_map/ppermute | solution.py:17
  138.5 2.6 copy-start.4
  149.5 1.2 copy-start.9
  152.3 4.2 collective-permute-start.7
  155.2 4.5 collective-permute-start.8
  159.9 5.2 collective-permute-start.10
  162.2 2.8 collective-permute-start.9
  170.1 5.0 collective-permute-start.12
  174.6 4.5 collective-permute-start.11
  188.7 2.6 copy-start.2
  199.7 1.1 copy-start.10
  203.0 3.0 collective-permute-start.13
  204.5 4.5 collective-permute-start.14
  209.2 8.0 collective-permute-start.16
  215.2 2.5 collective-permute-start.15
  222.7 4.0 collective-permute-start.18
  225.3 4.1 collective-permute-start.17
  238.9 2.6 copy-start.3
  252.7 1.1 copy-start.7
  252.7 3.0 copy-start.14
  254.7 48.0 %all-gather.7.cloned.1.call-start = ((), (), s32[]{:S(2)}) async-start(), calls=%async_computation.2 | async-start | bytes 1310720 | tf_op jit(solution)/shard_map/all_gather | solution.py:223
  255.7 561.4 %all-gather.9.cloned.1.call-start = ((), (), s32[]{:S(2)}) async-start(), calls=%async_computation.4 | async-start | bytes 7077888 | tf_op jit(solution)/shard_map/all_gather | solution.py:31
  305.5 614.3 %reduce-scatter.2.cloned.1.call-start = ((), (), s32[]{:S(2)}) async-start(), calls=%async_computation.3 | async-start | bytes 2433024 | tf_op jit(solution)/shard_map/reduce_scatter | solution.py:253
  841.3 1.3 copy-start.8
  842.6 77.2 %copy-start.1 = (f32[4,256]{1,0:T(4,128)S(1)}, f32[4,256]{1,0:T(4,128)}, u32[]{:S(2)}) copy-start(f32[4,256]{1,0:T(4,128)} %param.26) | copy-start | bytes 12292
  842.6 31.2 %collective-permute-start.19 = (f32[5,8,64,128]{3,2,1,0:T(8,128)S(1)}, f32[5,8,64,128]{3,2,1,0:T(8,128)S(1)}, u32[]{:S(2)}, u32[]{:S(2)}) collective-permute-start(f32[5,8,64,128]{3,2,1,0:T(8,128)S(1)} %copy-done.8), channel_id=1, source_target_pairs={{0,32},{32,64},{64,96},{1,33},{33,65},{65,97},{2,34},{34,66},{66,9... | collective-permute-start | bytes 3932168 | tf_op jit(solution)/shard_map/ppermute | solution.py:26
Sparse Core Ops, SparseCore 0:
  254.8 21.5 all-gather.4
  278.1 24.5 all-gather.6
  305.7 511.3 all-gather.8
  841.4 78.3 reduce-scatter.1
where the time goes:
time: 935 us; the launch traced here: 927 us
  waiting for transfers between devices  676 us (72%)
  other arithmetic  74.2 us (8%)
  blocking collectives  65.2 us (7%)
  local copies, waits for them, and re-layouts  58.3 us (6%)
  starting transfers between devices  35.9 us (4%)
  between operations  15.1 us (2%)
    all_gather x1, waiting for transfers between devices, entering(): everything = lax.all_gather(array, axis)  511 us
    pmax x1, blocking collectives, shards(): fastest = lax.pmax(wave_bound(shard_state), ('group', 'depth', 'image'))  65.2 us
    ppermute x2, waiting for transfers between devices, passed_along(): return lax.ppermute(block, axis, route)  52.3 us
    reduce_scatter x1, waiting for transfers between devices, shards(): lax.psum_scatter(arranged, ('group', 'depth'), scatter_dimension=0, tiled...  44.8 us
    all_gather x1, waiting for transfers between devices, shards(): lax.all_gather(safe_heat, 'group', axis=1, tiled=True)  26.3 us
    ppermute x9, starting transfers between devices, extended(): after = lax.ppermute(first, axis, down)  20.1 us
    all_gather x1, waiting for transfers between devices, shards(): lax.all_gather(safe_density, 'group', axis=1, tiled=True)  20 us
    concatenate x6, other arithmetic, extended(): array = jnp.concatenate([before, array, after], axis=dim)  19.8 us
  transfers between devices with their start and end apart: 24, of which 15 were waited for; matrix products, arithmetic and copies ran while one was open for 2% of the time, Pallas kernels for 0%

commit v1 on v0

v1 whole, which is shorter than its diff:
```python
import jax
import jax.numpy as jnp
from jax import lax
from jax.experimental import pallas as pl
from jax.experimental.pallas import tpu as pltpu
from jax.sharding import PartitionSpec as P

MESH = pl.DeviceIdType.MESH
HEAT_RATIO = 1.4
COURANT = 0.8
NG, ND, NI = 4, 8, 4
PZ, PX, PY = 8, 48, 128
NB = PX // 8
TOP = 8
PAIRS = [(g, i) for g in range(NG) for i in range(NI) if (g, i) != (0, 0)]


def take(table, index):
    return jnp.take_along_axis(table, index, axis=1, mode="promise_in_bounds")


def primitives(state):
    inverse = 1.0 / state[0]
    u, v, w = state[1] * inverse, state[2] * inverse, state[3] * inverse
    kinetic = 0.5 * (state[1] * u + state[2] * v + state[3] * w)
    p = (HEAT_RATIO - 1.0) * (state[4] - kinetic)
    return [u, v, w, p, jnp.sqrt(HEAT_RATIO * p * inverse)]


def flux(state, q, p, component):
    rows = [state[0] * q, state[1] * q, state[2] * q, state[3] * q, (state[4] + p) * q]
    rows[component] = rows[component] + p
    return rows


def kernel(
    density_in,
    velocity_in,
    pressure_in,
    palette_ref,
    index_ref,
    fluid_out,
    picture_out,
    raw,
    u_first,
    u_second,
    u_third,
    prim_a,
    prim_b,
    tend,
    x_send,
    x_recv,
    y_send,
    y_recv,
    y_part,
    max_own,
    max_line,
    max_mid,
    max_plane,
    fluid,
    shade,
    shade_index,
    tables,
    sheet,
    pair_recv,
    joined,
    chip_recv,
    picture,
    load_sem,
    store_sem,
    halo_send,
    halo_recv,
    line_send,
    line_recv,
    plane_send,
    plane_recv,
    pair_send_sem,
    pair_recv_sem,
    chip_send_sem,
    chip_recv_sem,
):
    g, d, i = lax.axis_index("group"), lax.axis_index("depth"), lax.axis_index("image")
    states = [u_first, u_second, u_third]
    prims = [prim_a, prim_b, prim_a]

    loads = [
        pltpu.make_async_copy(density_in, raw.at[0], load_sem.at[0]),
        pltpu.make_async_copy(velocity_in, raw.at[pl.ds(1, 3)], load_sem.at[1]),
        pltpu.make_async_copy(pressure_in, raw.at[4], load_sem.at[2]),
    ]
    for load in loads:
        load.start()

    barrier = pltpu.get_barrier_semaphore()
    for o in range(1, ND):
        pl.semaphore_signal(
            barrier, inc=1, device_id={"depth": lax.rem(d + o, ND)}, device_id_type=MESH
        )
    for og, oi in PAIRS:
        pl.semaphore_signal(
            barrier,
            inc=1,
            device_id={"group": lax.rem(g + og, NG), "image": lax.rem(i + oi, NI)},
            device_id_type=MESH,
        )

    lane = lax.broadcasted_iota(jnp.int32, (8, PY), 1)
    even = lax.rem(lane, 2) == 0
    at_first = lane == 0
    at_last = lane == PY - 1

    def pack_edges(s, z, r, new):
        rows = pl.ds(8 * r, 8)
        for c in range(5):
            shift = 16 * c + 2 * z
            turned = pltpu.roll(new[c], shift, 1)
            low = lax.rem(shift + PY - 1, PY)
            pltpu.store(
                y_send.at[s, rows, :], turned, mask=(lane == shift) | (lane == low)
            )
            if r == 0:
                x_send[s, 0, c, pl.ds(z, 1), :] = new[c][0:1]
            if r == NB - 1:
                x_send[s, 1, c, pl.ds(z, 1), :] = new[c][7:8]

    def put(s, z, r, new, derived):
        rows = pl.ds(TOP + 8 * r, 8)
        for c in range(5):
            states[s][c, z + 1, rows, :] = new[c]
            prims[s][c, z + 1, rows, :] = derived[c]
        pack_edges(s, z, r, new)

    def halo(s):
        up_d, down_d = lax.rem(d + 1, ND), lax.rem(d + ND - 1, ND)
        up_g, down_g = lax.rem(g + 1, NG), lax.rem(g + NG - 1, NG)
        up_i, down_i = lax.rem(i + 1, NI), lax.rem(i + NI - 1, NI)
        rows = pl.ds(TOP, PX)
        state = states[s]
        plan = [
            (state.at[:, 1, rows, :], state.at[:, PZ + 1, rows, :], {"depth": down_d}),
            (state.at[:, PZ, rows, :], state.at[:, 0, rows, :], {"depth": up_d}),
            (y_send.at[s], y_recv.at[s, 1], {"image": down_i}),
            (y_send.at[s], y_recv.at[s, 0], {"image": up_i}),
            (x_send.at[s, 0], x_recv.at[s, 1], {"group": down_g}),
            (x_send.at[s, 1], x_recv.at[s, 0], {"group": up_g}),
        ]
        return [
            pltpu.make_async_remote_copy(
                src_ref=src,
                dst_ref=dst,
                send_sem=halo_send.at[s, k],
                recv_sem=halo_recv.at[s, k],
                device_id=device,
                device_id_type=MESH,
            )
            for k, (src, dst, device) in enumerate(plan)
        ]

    def receive(s, copies):
        state, derived = states[s], prims[s]
        copies[4].wait_recv()
        copies[5].wait_recv()
        for side, wall, row in ((0, g == 0, TOP - 1), (1, g == NG - 1, TOP + PX)):
            cells = []
            for c in range(5):
                own = x_send[s, side, c]
                cells.append(jnp.where(wall, -own if c == 1 else own, x_recv[s, side, c]))
            values = primitives(cells)
            for c in range(5):
                for z in range(PZ):
                    state[c, z + 1, row : row + 1, :] = cells[c][z : z + 1]
                    derived[c, z + 1, row : row + 1, :] = values[c][z : z + 1]
        copies[2].wait_recv()
        copies[3].wait_recv()

        def edge(r, carry):
            rows = pl.ds(pl.multiple_of(8 * r, 8), 8)
            own, left, right = y_send[s, rows, :], y_recv[s, 0, rows, :], y_recv[s, 1, rows, :]
            inner, outer = [], []
            for c in range(5):
                inner.append(pltpu.roll(own, (PY - 16 * c) % PY, 1))
                outer.append(
                    jnp.where(
                        even,
                        pltpu.roll(left, (PY + 1 - 16 * c) % PY, 1),
                        pltpu.roll(right, (PY - 1 - 16 * c) % PY, 1),
                    )
                )
            prim_in, prim_out = primitives(inner), primitives(outer)
            fastest = jnp.maximum(
                jnp.abs(prim_in[1]) + prim_in[4], jnp.abs(prim_out[1]) + prim_out[4]
            )
            flows = flux(outer, prim_out[1], prim_out[3], 2)
            for c in range(5):
                y_part[c, rows, :] = jnp.where(even, flows[c], -flows[c]) + fastest * (
                    outer[c] - inner[c]
                )
            return carry

        lax.fori_loop(0, NB, edge, 0)
        copies[0].wait_recv()
        copies[1].wait_recv()

        def plane(r, carry):
            rows = pl.ds(pl.multiple_of(TOP + 8 * r, 8), 8)
            for z in (0, PZ + 1):
                values = primitives([state[c, z, rows, :] for c in range(5)])
                for c in range(5):
                    derived[c, z, rows, :] = values[c]
            return carry

        lax.fori_loop(0, NB, plane, 0)

    def twice_tendency(s, z, r):
        state, derived = states[s], prims[s]
        row = TOP + 8 * r
        cell = [state[c, z + 1, row : row + 8, :] for c in range(5)]
        prim = [derived[c, z + 1, row : row + 8, :] for c in range(5)]
        total = [None] * 5
        for axis, component in ((0, 3), (1, 1)):
            here = jnp.abs(prim[component - 1]) + prim[4]
            for side in (-1, 1):
                zz = z + 1 + (side if axis == 0 else 0)
                rr = row + (side if axis == 1 else 0)
                near = [state[c, zz, rr : rr + 8, :] for c in range(5)]
                q = derived[component - 1, zz, rr : rr + 8, :]
                p = derived[3, zz, rr : rr + 8, :]
                fastest = jnp.maximum(here, jnp.abs(q) + derived[4, zz, rr : rr + 8, :])
                flows = flux(near, q, p, component)
                for c in range(5):
                    part = fastest * (near[c] - cell[c])
                    part = part + flows[c] if side < 0 else part - flows[c]
                    total[c] = part if total[c] is None else total[c] + part
        here = jnp.abs(prim[1]) + prim[4]
        turn = lax.rem(PY - 2 * z, PY)
        edges = [pltpu.roll(y_part[c, 8 * r : 8 * r + 8, :], turn, 1) for c in range(5)]
        for side in (-1, 1):
            shift = 1 if side < 0 else PY - 1
            near = [pltpu.roll(cell[c], shift, 1) for c in range(5)]
            q, p = pltpu.roll(prim[1], shift, 1), pltpu.roll(prim[3], shift, 1)
            fastest = jnp.maximum(here, pltpu.roll(here, shift, 1))
            flows = flux(near, q, p, 2)
            for c in range(5):
                part = fastest * (near[c] - cell[c])
                part = part + flows[c] if side < 0 else part - flows[c]
                total[c] = total[c] + jnp.where(at_first if side < 0 else at_last, edges[c], part)
        return total

    for load in loads:
        load.wait()

    def first(z, most):
        for r in range(NB):
            rho, u, v, w, p = [raw[c, z, 8 * r : 8 * r + 8, :] for c in range(5)]
            energy = p / (HEAT_RATIO - 1.0) + 0.5 * rho * (u * u + v * v + w * w)
            sound = jnp.sqrt(HEAT_RATIO * p / rho)
            put(0, z, r, [rho, rho * u, rho * v, rho * w, energy], [u, v, w, p, sound])
            most = jnp.maximum(most, jnp.abs(u) + jnp.abs(v) + jnp.abs(w) + 3.0 * sound)
        return most

    max_own[...] = lax.fori_loop(0, PZ, first, jnp.zeros((8, PY), jnp.float32))
    pl.semaphore_wait(barrier, ND - 1 + len(PAIRS))

    lines = [
        pltpu.make_async_remote_copy(
            src_ref=max_own,
            dst_ref=max_line.at[o - 1],
            send_sem=line_send.at[o - 1],
            recv_sem=line_recv.at[o - 1],
            device_id={"depth": lax.rem(d + o, ND)},
            device_id_type=MESH,
        )
        for o in range(1, ND)
    ]
    for copy in lines:
        copy.start()
    halos = [halo(0)]
    for copy in halos[0]:
        copy.start()
    for copy in lines:
        copy.wait_recv()
    most = max_own[...]
    for o in range(ND - 1):
        most = jnp.maximum(most, max_line[o])
    max_mid[...] = most
    planes = [
        pltpu.make_async_remote_copy(
            src_ref=max_mid,
            dst_ref=max_plane.at[k],
            send_sem=plane_send.at[k],
            recv_sem=plane_recv.at[k],
            device_id={"group": lax.rem(g + og, NG), "image": lax.rem(i + oi, NI)},
            device_id_type=MESH,
        )
        for k, (og, oi) in enumerate(PAIRS)
    ]
    for copy in planes:
        copy.start()

    pick = lax.rem(2 * lane, PY)
    low, high = index_ref[:, 0:PY], index_ref[:, PY : 2 * PY]
    half = lane < PY // 2
    bins = [
        jnp.where(half, take(low, pick + k), take(high, pick + k)) for k in range(2)
    ]
    for c in range(4):
        pal_low = jnp.broadcast_to(palette_ref[c : c + 1, 0:PY], (8, PY))
        pal_high = jnp.broadcast_to(palette_ref[c : c + 1, PY : 2 * PY], (8, PY))
        colours = []
        for b in bins:
            within = b & (PY - 1)
            colours.append(jnp.where(b < PY, take(pal_low, within), take(pal_high, within)))
        after = pltpu.roll(colours[0], PY - 1, 1)
        tables[3 * c] = colours[0]
        tables[3 * c + 1] = colours[1] - colours[0]
        tables[3 * c + 2] = after - colours[1]

    receive(0, halos[0])

    def tend_plane(z, carry):
        for r in range(NB):
            total = twice_tendency(0, z, r)
            for c in range(5):
                tend[c, z, 8 * r : 8 * r + 8, :] = total[c]
        return carry

    lax.fori_loop(0, PZ, tend_plane, 0)

    for copy in planes:
        copy.wait_recv()
    most = max_mid[...]
    for k in range(len(PAIRS)):
        most = jnp.maximum(most, max_plane[k])
    half_step = (0.5 * COURANT) / jnp.broadcast_to(
        jnp.max(most, axis=(0, 1), keepdims=True), (8, PY)
    )

    def section_one(z, carry):
        for r in range(NB):
            new = [
                u_first[c, z + 1, TOP + 8 * r : TOP + 8 * r + 8, :]
                + half_step * tend[c, z, 8 * r : 8 * r + 8, :]
                for c in range(5)
            ]
            put(1, z, r, new, primitives(new))
        return carry

    lax.fori_loop(0, PZ, section_one, 0)
    halos.append(halo(1))
    for copy in halos[1]:
        copy.start()
    receive(1, halos[1])

    def section_two(z, carry):
        for r in range(NB):
            total = twice_tendency(1, z, r)
            row = TOP + 8 * r
            new = [
                0.75 * u_first[c, z + 1, row : row + 8, :]
                + 0.25 * (u_second[c, z + 1, row : row + 8, :] + half_step * total[c])
                for c in range(5)
            ]
            put(2, z, r, new, primitives(new))
        return carry

    lax.fori_loop(0, PZ, section_two, 0)
    halos.append(halo(2))
    for copy in halos[2]:
        copy.start()
    receive(2, halos[2])

    def section_three(z, carry):
        for r in range(NB):
            total = twice_tendency(2, z, r)
            row = TOP + 8 * r
            rows = slice(8 * r, 8 * r + 8)
            new = [
                u_first[c, z + 1, row : row + 8, :] * (1.0 / 3.0)
                + (2.0 / 3.0) * (u_third[c, z + 1, row : row + 8, :] + half_step * total[c])
                for c in range(5)
            ]
            for c in range(5):
                fluid[c, z, rows, :] = new[c]
            inverse = 1.0 / new[0]
            kinetic = 0.5 * inverse * (new[1] * new[1] + new[2] * new[2] + new[3] * new[3])
            position = jnp.clip(new[0] - 0.5, 0.0, 1.0) * 255.0
            index = (position * 0.5).astype(jnp.int32)
            past = position - 2.0 * index.astype(jnp.float32)
            shade_index[z, rows, :] = index
            shade[0, z, rows, :] = jnp.minimum(past, 1.0)
            shade[1, z, rows, :] = jnp.maximum(past - 1.0, 0.0)
            shade[2, z, rows, :] = new[0] * (-2.0 / (PZ * ND))
            shade[3, z, rows, :] = (HEAT_RATIO - 1.0) * (new[4] - kinetic) * inverse
        return carry

    lax.fori_loop(0, PZ, section_three, 0)
    fluid_store = pltpu.make_async_copy(fluid, fluid_out, store_sem.at[0])
    fluid_store.start()

    chip, core = d // 2, lax.rem(d, 2)

    def render(t):
        rows_of = [
            jnp.broadcast_to(tables[k, pl.ds(t, 1), :], (8, PY)) for k in range(12)
        ]

        def block(r, carry):
            rows = pl.ds(pl.multiple_of(8 * r, 8), 8)
            clear = jnp.ones((8, PY), jnp.float32)
            light = [jnp.zeros((8, PY), jnp.float32) for _ in range(3)]
            for z in range(PZ):
                index = shade_index[z, rows, :]
                one, two = shade[0, z, rows, :], shade[1, z, rows, :]
                looked = [
                    take(rows_of[3 * c], index)
                    + one * take(rows_of[3 * c + 1], index)
                    + two * take(rows_of[3 * c + 2], index)
                    for c in range(4)
                ]
                through = jnp.exp(looked[3] * shade[2, z, rows, :])
                weight = clear * (1.0 - through) * shade[3, z, rows, :]
                light = [light[c] + weight * looked[c] for c in range(3)]
                clear = clear * through
            sheet[t, 0, rows, :] = clear
            for c in range(3):
                sheet[t, c + 1, rows, :] = light[c]
            return carry

        lax.fori_loop(0, NB, block, 0)

    pair_copies, chip_copies = [], []
    for k in range(4):
        t = 2 * lax.rem(chip + 2 + k, 4) + (1 - core)
        slot = lax.rem(chip + 2 + k, 4)
        render(t)
        copy = pltpu.make_async_remote_copy(
            src_ref=sheet.at[t],
            dst_ref=pair_recv.at[slot],
            send_sem=pair_send_sem.at[slot],
            recv_sem=pair_recv_sem.at[slot],
            device_id={"depth": 2 * chip + 1 - core},
            device_id_type=MESH,
        )
        copy.start()
        pair_copies.append(copy)
    front = core == 0
    for k, offset in enumerate((2, 3, 1, 0)):
        owner = lax.rem(chip + offset, 4)
        t = 2 * owner + core
        render(t)
        pltpu.make_async_remote_copy(
            src_ref=sheet.at[t],
            dst_ref=pair_recv.at[owner],
            send_sem=pair_send_sem.at[owner],
            recv_sem=pair_recv_sem.at[owner],
            device_id={"depth": 2 * chip + 1 - core},
            device_id_type=MESH,
        ).wait_recv()
        own_clear, other_clear = sheet[t, 0], pair_recv[owner, 0]
        own_scale = jnp.where(front, 1.0, other_clear)
        other_scale = jnp.where(front, own_clear, 1.0)
        target = chip_recv.at[chip] if offset == 0 else joined.at[owner]
        target[0] = own_clear * other_clear
        for c in range(1, 4):
            target[c] = own_scale * sheet[t, c] + other_scale * pair_recv[owner, c]
        if offset != 0:
            copy = pltpu.make_async_remote_copy(
                src_ref=joined.at[owner],
                dst_ref=chip_recv.at[chip],
                send_sem=chip_send_sem.at[owner],
                recv_sem=chip_recv_sem.at[chip],
                device_id={"depth": t},
                device_id_type=MESH,
            )
            copy.start()
            chip_copies.append(copy)
    for offset in (1, 3, 2):
        source = lax.rem(chip + offset, 4)
        pltpu.make_async_remote_copy(
            src_ref=joined.at[source],
            dst_ref=chip_recv.at[source],
            send_sem=chip_send_sem.at[source],
            recv_sem=chip_recv_sem.at[source],
            device_id={"depth": 2 * source + core},
            device_id_type=MESH,
        ).wait_recv()
    ahead = chip_recv[0, 0]
    light = [chip_recv[0, c] for c in range(1, 4)]
    for k in range(1, 4):
        for c in range(3):
            light[c] = light[c] + ahead * chip_recv[k, c + 1]
        if k < 3:
            ahead = ahead * chip_recv[k, 0]
    for c in range(3):
        picture[c] = light[c]
    picture_store = pltpu.make_async_copy(picture, picture_out, store_sem.at[1])
    picture_store.start()

    for copy in lines + planes + halos[0] + halos[1] + halos[2] + pair_copies + chip_copies:
        copy.wait_send()
    fluid_store.wait()
    picture_store.wait()


def shards(density, velocity, pressure, palette, palette_index):
    f32 = jnp.float32
    any_space = pl.BlockSpec(memory_space=pl.ANY)
    vmem = pl.BlockSpec(memory_space=pltpu.VMEM)
    padded = (5, PZ + 2, PX + 16, PY)
    dma = pltpu.SemaphoreType.DMA
    fluid_state, picture = pl.pallas_call(
        kernel,
        out_shape=(
            jax.ShapeDtypeStruct((5, PZ, PX, PY), f32),
            jax.ShapeDtypeStruct((3, PX, PY), f32),
        ),
        in_specs=[any_space, any_space, any_space, vmem, vmem],
        out_specs=(any_space, any_space),
        scratch_shapes=[
            pltpu.VMEM((5, PZ, PX, PY), f32),
            pltpu.VMEM(padded, f32),
            pltpu.VMEM(padded, f32),
            pltpu.VMEM(padded, f32),
            pltpu.VMEM(padded, f32),
            pltpu.VMEM(padded, f32),
            pltpu.VMEM((5, PZ, PX, PY), f32),
            pltpu.VMEM((3, 2, 5, PZ, PY), f32),
            pltpu.VMEM((3, 2, 5, PZ, PY), f32),
            pltpu.VMEM((3, PX, PY), f32),
            pltpu.VMEM((3, 2, PX, PY), f32),
            pltpu.VMEM((5, PX, PY), f32),
            pltpu.VMEM((8, PY), f32),
            pltpu.VMEM((ND - 1, 8, PY), f32),
            pltpu.VMEM((8, PY), f32),
            pltpu.VMEM((len(PAIRS), 8, PY), f32),
            pltpu.VMEM((5, PZ, PX, PY), f32),
            pltpu.VMEM((4, PZ, PX, PY), f32),
            pltpu.VMEM((PZ, PX, PY), jnp.int32),
            pltpu.VMEM((12, 8, PY), f32),
            pltpu.VMEM((8, 4, PX, PY), f32),
            pltpu.VMEM((4, 4, PX, PY), f32),
            pltpu.VMEM((4, 4, PX, PY), f32),
            pltpu.VMEM((4, 4, PX, PY), f32),
            pltpu.VMEM((3, PX, PY), f32),
            dma((3,)),
            dma((2,)),
            dma((3, 6)),
            dma((3, 6)),
            dma((ND - 1,)),
            dma((ND - 1,)),
            dma((len(PAIRS),)),
            dma((len(PAIRS),)),
            dma((4,)),
            dma((4,)),
            dma((4,)),
            dma((4,)),
        ],
        compiler_params=pltpu.CompilerParams(
            collective_id=0, has_side_effects=True, vmem_limit_bytes=40 * 1024 * 1024
        ),
    )(density, velocity, pressure, palette, palette_index)
    return fluid_state, picture[None]


def solution(mesh):
    return jax.shard_map(
        shards,
        mesh=mesh,
        in_specs=(
            P("depth", "group", "image"),
            P(None, "depth", "group", "image"),
            P("depth", "group", "image"),
            P(),
            P(),
        ),
        out_specs=(P(None, "depth", "group", "image"), P("depth", None, "group", "image")),
        check_vma=False,
    )
```

time: 935 us -> 53.5 us (0.06)
  waiting for transfers between devices: 676 us -> 0 us
  other arithmetic: 74.2 us -> 0 us
  blocking collectives: 65.2 us -> 0 us
  local copies, waits for them, and re-layouts: 58.3 us -> 5.87 us
  Pallas kernels: 0 us -> 46.7 us
  starting transfers between devices: 35.9 us -> 0 us
  between operations: 15.1 us -> 0.65 us
    all_gather x3 -> x0, waiting for transfers between devices: 558 us -> none  [the longest x1 511 us: entering(): everything = lax.all_gather(array, axis)]
    ppermute x20 -> x0, waiting for transfers between devices: 73.3 us -> none  [the longest x2 52.3 us: passed_along(): return lax.ppermute(block, axis, route)]
    pmax x1 -> x0, blocking collectives: 65.2 us -> none  [shards(): fastest = lax.pmax(wave_bound(shard_state), ('group', 'depth', 'image'))]
    pallas_call x0 -> x1, Pallas kernels: none -> 46.7 us  [shards(): pl.pallas_call(kernel, out_shape=(jax.ShapeDtypeStruct((5, PZ, PX, PY), f...]
    reduce_scatter x1 -> x0, waiting for transfers between devices: 44.8 us -> none  [shards(): lax.psum_scatter(arranged, ('group', 'depth'), scatter_dimension=0, tiled...]
    ppermute x20 -> x0, starting transfers between devices: 35.7 us -> none  [the longest x9 20.1 us: extended(): after = lax.ppermute(first, axis, down)]
    concatenate x9 -> x0, other arithmetic: 21.3 us -> none  [the longest x6 19.8 us: extended(): array = jnp.concatenate([before, array, after], axis=dim)]
    unnamed x29 -> x12, local copies, waits for them, and re-layouts: 19 us -> 5.87 us
  transfers between devices with their start and end apart: 24 -> 0, of which waited for: 15 -> 0; matrix products, arithmetic and copies ran while one was open for 2% -> 0% of each run, Pallas kernels for 0% -> 0%
where the time goes in v1:
time: 53.5 us; the launch traced here: 53.3 us
  Pallas kernels  46.7 us (87%)
  local copies, waits for them, and re-layouts  5.87 us (11%)
  between operations  0.65 us (1%)
    pallas_call x1, Pallas kernels, shards(): pl.pallas_call(kernel, out_shape=(jax.ShapeDtypeStruct((5, PZ, PX, PY), f...  46.7 us
    unnamed x12, local copies, waits for them, and re-layouts  5.87 us

profile of v1, /device:TPU:1, one launch (start us, length us, event | category | flops | bytes accessed | tf_op | source)
XLA Modules:
  0.0 53.3 jit_solution(11376794366479809400)
XLA Ops:
  0.6 0.0 copy-start
  0.6 1.1 %copy-done = f32[3,8,48,128]{3,2,1,0:T(8,128)S(1)} copy-done((f32[3,8,48,128]{3,2,1,0:T(8,128)S(1)}, f32[3,8,48,128]{3,2,1,0:T(8,128)}, u32[]{:S(2)}) %copy-start) | copy-done | bytes 589848
  1.7 0.0 copy-start.1
  1.7 0.9 %copy-done.1 = f32[8,48,128]{2,1,0:T(8,128)S(1)} copy-done((f32[8,48,128]{2,1,0:T(8,128)S(1)}, f32[8,48,128]{2,1,0:T(8,128)}, u32[]{:S(2)}) %copy-start.1) | copy-done | bytes 196632
  2.6 0.0 copy-start.2
  2.6 0.9 %copy-done.2 = f32[8,48,128]{2,1,0:T(8,128)S(1)} copy-done((f32[8,48,128]{2,1,0:T(8,128)S(1)}, f32[8,48,128]{2,1,0:T(8,128)}, u32[]{:S(2)}) %copy-start.2) | copy-done | bytes 196632
  3.6 0.0 copy-start.3
  3.6 0.7 %copy-done.3 = s32[8,256]{1,0:T(8,128)S(1)} copy-done((s32[8,256]{1,0:T(8,128)S(1)}, s32[8,256]{1,0:T(8,128)}, u32[]{:S(2)}) %copy-start.3) | copy-done | bytes 8216
  4.2 0.0 copy-start.4
  4.3 0.7 %copy-done.4 = f32[4,256]{1,0:T(4,128)S(1)} copy-done((f32[4,256]{1,0:T(4,128)S(1)}, f32[4,256]{1,0:T(4,128)}, u32[]{:S(2)}) %copy-start.4) | copy-done | bytes 4120
  4.9 46.7 %shard_map.68 = (f32[5,8,48,128]{3,2,1,0:T(8,128)S(1)}, f32[3,48,128]{2,1,0:T(8,128)S(1)}) custom-call(f32[8,48,128]{2,1,0:T(8,128)S(1)} %copy-done.1, f32[3,8,48,128]{3,2,1,0:T(8,128)S(1)} %copy-done, f32[8,48,128]{2,1,0:T(8,128)S(1)} %copy-done.2, f32[4,256]{1,0:T(4,128)S(1)} %copy-done.4, s32[8,256]{1,0:T(8,128)S(1)} %copy-done.3), custom_call_target="tpu_custom_call" | custom-call | tf_op jit(solution)/shard_map/pallas_call | solution.py:511
  51.7 0.9 %copy.9 = f32[5,8,48,128]{3,2,1,0:T(8,128)} copy(f32[5,8,48,128]{3,2,1,0:T(8,128)S(1)} %get-tuple-element.8) | data formatting | bytes 1966080
  52.6 0.6 %copy.10 = f32[1,3,48,128]{3,2,1,0:T(8,128)} copy(f32[1,3,48,128]{3,2,1,0:T(8,128)S(1)} %bitcast.1) | data formatting | bytes 147456
Async XLA Ops:
  0.6 1.1 %copy-start = (f32[3,8,48,128]{3,2,1,0:T(8,128)S(1)}, f32[3,8,48,128]{3,2,1,0:T(8,128)}, u32[]{:S(2)}) copy-start(f32[3,8,48,128]{3,2,1,0:T(8,128)} %velocity_in.1) | copy-start | bytes 1769476
  1.7 0.9 %copy-start.1 = (f32[8,48,128]{2,1,0:T(8,128)S(1)}, f32[8,48,128]{2,1,0:T(8,128)}, u32[]{:S(2)}) copy-start(f32[8,48,128]{2,1,0:T(8,128)} %density_in.1) | copy-start | bytes 589828
  2.6 0.9 %copy-start.2 = (f32[8,48,128]{2,1,0:T(8,128)S(1)}, f32[8,48,128]{2,1,0:T(8,128)}, u32[]{:S(2)}) copy-start(f32[8,48,128]{2,1,0:T(8,128)} %pressure_in.1) | copy-start | bytes 589828
  3.6 0.7 %copy-start.3 = (s32[8,256]{1,0:T(8,128)S(1)}, s32[8,256]{1,0:T(8,128)}, u32[]{:S(2)}) copy-start(s32[8,256]{1,0:T(8,128)} %index_ref.1) | copy-start | bytes 24580
  4.2 0.7 %copy-start.4 = (f32[4,256]{1,0:T(4,128)S(1)}, f32[4,256]{1,0:T(4,128)}, u32[]{:S(2)}) copy-start(f32[4,256]{1,0:T(4,128)} %palette_ref.1) | copy-start | bytes 12292

commit v2 on v1

--- a/solution.py
+++ b/solution.py
@@ -12,6 +12,7 @@
 PZ, PX, PY = 8, 48, 128
 NB = PX // 8
 TOP = 8
+STEP = 2.0 / 65535.0
 PAIRS = [(g, i) for g in range(NG) for i in range(NI) if (g, i) != (0, 0)]
 
 
@@ -37,11 +38,13 @@
     density_in,
     velocity_in,
     pressure_in,
-    palette_ref,
-    index_ref,
+    palette_in,
+    index_in,
     fluid_out,
     picture_out,
     raw,
+    palette_ref,
+    index_ref,
     u_first,
     u_second,
     u_third,
@@ -74,6 +77,7 @@
     line_recv,
     plane_send,
     plane_recv,
+    token,
     pair_send_sem,
     pair_recv_sem,
     chip_send_sem,
@@ -87,6 +91,8 @@
         pltpu.make_async_copy(density_in, raw.at[0], load_sem.at[0]),
         pltpu.make_async_copy(velocity_in, raw.at[pl.ds(1, 3)], load_sem.at[1]),
         pltpu.make_async_copy(pressure_in, raw.at[4], load_sem.at[2]),
+        pltpu.make_async_copy(palette_in, palette_ref, load_sem.at[3]),
+        pltpu.make_async_copy(index_in, index_ref, load_sem.at[4]),
     ]
     for load in loads:
         load.start()
@@ -96,12 +102,13 @@
         pl.semaphore_signal(
             barrier, inc=1, device_id={"depth": lax.rem(d + o, ND)}, device_id_type=MESH
         )
-    for og, oi in PAIRS:
+    for o in range(1, NG):
         pl.semaphore_signal(
-            barrier,
-            inc=1,
-            device_id={"group": lax.rem(g + og, NG), "image": lax.rem(i + oi, NI)},
-            device_id_type=MESH,
+            barrier, inc=1, device_id={"group": lax.rem(g + o, NG)}, device_id_type=MESH
+        )
+    for o in range(1, NI):
+        pl.semaphore_signal(
+            barrier, inc=1, device_id={"image": lax.rem(i + o, NI)}, device_id_type=MESH
         )
 
     lane = lax.broadcasted_iota(jnp.int32, (8, PY), 1)
@@ -246,7 +253,7 @@
                 total[c] = total[c] + jnp.where(at_first if side < 0 else at_last, edges[c], part)
         return total
 
-    for load in loads:
+    for load in loads[:3]:
         load.wait()
 
     def first(z, most):
@@ -259,8 +266,12 @@
         return most
 
     max_own[...] = lax.fori_loop(0, PZ, first, jnp.zeros((8, PY), jnp.float32))
-    pl.semaphore_wait(barrier, ND - 1 + len(PAIRS))
-
+    pl.semaphore_wait(barrier, ND + NG + NI - 3)
+
+    for o in range(1, NI):
+        pl.semaphore_signal(
+            token, inc=1, device_id={"image": lax.rem(i + o, NI)}, device_id_type=MESH
+        )
     lines = [
         pltpu.make_async_remote_copy(
             src_ref=max_own,
@@ -294,26 +305,32 @@
         )
         for k, (og, oi) in enumerate(PAIRS)
     ]
+    pl.semaphore_wait(token, NI - 1)
     for copy in planes:
         copy.start()
 
+    for load in loads[3:]:
+        load.wait()
     pick = lax.rem(2 * lane, PY)
     low, high = index_ref[:, 0:PY], index_ref[:, PY : 2 * PY]
     half = lane < PY // 2
     bins = [
         jnp.where(half, take(low, pick + k), take(high, pick + k)) for k in range(2)
     ]
+    words = []
     for c in range(4):
         pal_low = jnp.broadcast_to(palette_ref[c : c + 1, 0:PY], (8, PY))
         pal_high = jnp.broadcast_to(palette_ref[c : c + 1, PY : 2 * PY], (8, PY))
-        colours = []
+        levels = []
         for b in bins:
             within = b & (PY - 1)
-            colours.append(jnp.where(b < PY, take(pal_low, within), take(pal_high, within)))
-        after = pltpu.roll(colours[0], PY - 1, 1)
-        tables[3 * c] = colours[0]
-        tables[3 * c + 1] = colours[1] - colours[0]
-        tables[3 * c + 2] = after - colours[1]
+            colour = jnp.where(b < PY, take(pal_low, within), take(pal_high, within))
+            levels.append((colour * (1.0 / STEP) + 0.5).astype(jnp.int32))
+        levels.append(pltpu.roll(levels[0], PY - 1, 1))
+        words.append(levels)
+    for k in range(3):
+        for c in range(2):
+            tables[2 * k + c] = (words[c][k] - 32768) * 65536 + words[c + 2][k]
 
     receive(0, halos[0])
 
@@ -387,10 +404,10 @@
             index = (position * 0.5).astype(jnp.int32)
             past = position - 2.0 * index.astype(jnp.float32)
             shade_index[z, rows, :] = index
-            shade[0, z, rows, :] = jnp.minimum(past, 1.0)
+            shade[0, z, rows, :] = 1.0 - jnp.minimum(past, 1.0)
             shade[1, z, rows, :] = jnp.maximum(past - 1.0, 0.0)
-            shade[2, z, rows, :] = new[0] * (-2.0 / (PZ * ND))
-            shade[3, z, rows, :] = (HEAT_RATIO - 1.0) * (new[4] - kinetic) * inverse
+            shade[2, z, rows, :] = new[0] * (-2.0 * STEP / (PZ * ND))
+            shade[3, z, rows, :] = (STEP * (HEAT_RATIO - 1.0)) * (new[4] - kinetic) * inverse
         return carry
 
     lax.fori_loop(0, PZ, section_three, 0)
@@ -401,89 +418,95 @@
 
     def render(t):
         rows_of = [
-            jnp.broadcast_to(tables[k, pl.ds(t, 1), :], (8, PY)) for k in range(12)
+            jnp.broadcast_to(tables[k, pl.ds(t, 1), :], (8, PY)) for k in range(6)
         ]
-
-        def block(r, carry):
-            rows = pl.ds(pl.multiple_of(8 * r, 8), 8)
-            clear = jnp.ones((8, PY), jnp.float32)
-            light = [jnp.zeros((8, PY), jnp.float32) for _ in range(3)]
+        for r in range(NB):
+            rows = slice(8 * r, 8 * r + 8)
+            clear, light = None, None
             for z in range(PZ):
                 index = shade_index[z, rows, :]
-                one, two = shade[0, z, rows, :], shade[1, z, rows, :]
-                looked = [
-                    take(rows_of[3 * c], index)
-                    + one * take(rows_of[3 * c + 1], index)
-                    + two * take(rows_of[3 * c + 2], index)
-                    for c in range(4)
-                ]
+                scale = [shade[0, z, rows, :], None, shade[1, z, rows, :]]
+                scale[1] = 1.0 - scale[0] - scale[2]
+                looked = [None] * 4
+                for k in range(3):
+                    for c in range(2):
+                        word = take(rows_of[2 * k + c], index)
+                        upper = (word >> 16).astype(jnp.float32) * scale[k]
+                        lower = (word & 65535).astype(jnp.float32) * scale[k]
+                        looked[c] = upper if k == 0 else looked[c] + upper
+                        looked[c + 2] = lower if k == 0 else looked[c + 2] + lower
+                looked[0] = looked[0] + 32768.0
+                looked[1] = looked[1] + 32768.0
                 through = jnp.exp(looked[3] * shade[2, z, rows, :])
-                weight = clear * (1.0 - through) * shade[3, z, rows, :]
-                light = [light[c] + weight * looked[c] for c in range(3)]
-                clear = clear * through
+                weight = (1.0 - through) * shade[3, z, rows, :]
+                if z == 0:
+                    light = [weight * looked[c] for c in range(3)]
+                    clear = through
+                else:
+                    weight = weight * clear
+                    light = [light[c] + weight * looked[c] for c in range(3)]
+                    clear = clear * through
             sheet[t, 0, rows, :] = clear
             for c in range(3):
                 sheet[t, c + 1, rows, :] = light[c]
-            return carry
-
-        lax.fori_loop(0, NB, block, 0)
-
-    pair_copies, chip_copies = [], []
-    for k in range(4):
-        t = 2 * lax.rem(chip + 2 + k, 4) + (1 - core)
-        slot = lax.rem(chip + 2 + k, 4)
-        render(t)
-        copy = pltpu.make_async_remote_copy(
-            src_ref=sheet.at[t],
+
+    def pair_copy(slot):
+        return pltpu.make_async_remote_copy(
+            src_ref=sheet.at[2 * slot + 1 - core],
             dst_ref=pair_recv.at[slot],
             send_sem=pair_send_sem.at[slot],
             recv_sem=pair_recv_sem.at[slot],
             device_id={"depth": 2 * chip + 1 - core},
             device_id_type=MESH,
         )
-        copy.start()
-        pair_copies.append(copy)
-    front = core == 0
-    for k, offset in enumerate((2, 3, 1, 0)):
+
+    def chip_copy(owner, source):
+        return pltpu.make_async_remote_copy(
+            src_ref=joined.at[owner],
+            dst_ref=chip_recv.at[source],
+            send_sem=chip_send_sem.at[owner],
+            recv_sem=chip_recv_sem.at[source],
+            device_id={"depth": 2 * owner + core},
+            device_id_type=MESH,
+        )
+
+    def turn(k, carry):
+        mine = (k == 3) | (k == 4) | (k == 5) | (k == 7)
+        offset = jnp.where(k < 6, 1 + lax.rem(k + 1, 3), 0)
         owner = lax.rem(chip + offset, 4)
-        t = 2 * owner + core
+        t = 2 * owner + jnp.where(mine, core, 1 - core)
         render(t)
-        pltpu.make_async_remote_copy(
-            src_ref=sheet.at[t],
-            dst_ref=pair_recv.at[owner],
-            send_sem=pair_send_sem.at[owner],
-            recv_sem=pair_recv_sem.at[owner],
-            device_id={"depth": 2 * chip + 1 - core},
-            device_id_type=MESH,
-        ).wait_recv()
-        own_clear, other_clear = sheet[t, 0], pair_recv[owner, 0]
-        own_scale = jnp.where(front, 1.0, other_clear)
-        other_scale = jnp.where(front, own_clear, 1.0)
-        target = chip_recv.at[chip] if offset == 0 else joined.at[owner]
-        target[0] = own_clear * other_clear
-        for c in range(1, 4):
-            target[c] = own_scale * sheet[t, c] + other_scale * pair_recv[owner, c]
-        if offset != 0:
-            copy = pltpu.make_async_remote_copy(
-                src_ref=joined.at[owner],
-                dst_ref=chip_recv.at[chip],
-                send_sem=chip_send_sem.at[owner],
-                recv_sem=chip_recv_sem.at[chip],
-                device_id={"depth": t},
-                device_id_type=MESH,
-            )
-            copy.start()
-            chip_copies.append(copy)
-    for offset in (1, 3, 2):
-        source = lax.rem(chip + offset, 4)
-        pltpu.make_async_remote_copy(
-            src_ref=joined.at[source],
-            dst_ref=chip_recv.at[source],
-            send_sem=chip_send_sem.at[source],
-            recv_sem=chip_recv_sem.at[source],
-            device_id={"depth": 2 * source + core},
-            device_id_type=MESH,
-        ).wait_recv()
+
+        @pl.when(jnp.logical_not(mine))
+        def _():
+            pair_copy(owner).start()
+
+        @pl.when(mine)
+        def _():
+            pair_copy(owner).wait_recv()
+            for r in range(NB):
+                rows = slice(8 * r, 8 * r + 8)
+                own_clear, other_clear = sheet[t, 0, rows, :], pair_recv[owner, 0, rows, :]
+                own_scale = jnp.where(core == 0, 1.0, other_clear)
+                other_scale = jnp.where(core == 0, own_clear, 1.0)
+                joined[owner, 0, rows, :] = own_clear * other_clear
+                for c in range(1, 4):
+                    joined[owner, c, rows, :] = (
+                        own_scale * sheet[t, c, rows, :]
+                        + other_scale * pair_recv[owner, c, rows, :]
+                    )
+
+        @pl.when(mine & (k < 6))
+        def _():
+            chip_copy(owner, chip).start()
+
+        return carry
+
+    lax.fori_loop(0, 8, turn, 0)
+    for o in (1, 3, 2):
+        source = lax.rem(chip + o, 4)
+        chip_copy(source, source).wait_recv()
+    chip_recv[chip] = joined[chip]
     ahead = chip_recv[0, 0]
     light = [chip_recv[0, c] for c in range(1, 4)]
     for k in range(1, 4):
@@ -496,8 +519,13 @@
     picture_store = pltpu.make_async_copy(picture, picture_out, store_sem.at[1])
     picture_store.start()
 
-    for copy in lines + planes + halos[0] + halos[1] + halos[2] + pair_copies + chip_copies:
+    for copy in lines + planes + halos[0] + halos[1] + halos[2]:
         copy.wait_send()
+    for k in range(4):
+        pair_copy(k).wait_send()
+    for o in range(1, 4):
+        source = lax.rem(chip + o, 4)
+        chip_copy(source, source).wait_send()
     fluid_store.wait()
     picture_store.wait()
 
@@ -505,7 +533,6 @@
 def shards(density, velocity, pressure, palette, palette_index):
     f32 = jnp.float32
     any_space = pl.BlockSpec(memory_space=pl.ANY)
-    vmem = pl.BlockSpec(memory_space=pltpu.VMEM)
     padded = (5, PZ + 2, PX + 16, PY)
     dma = pltpu.SemaphoreType.DMA
     fluid_state, picture = pl.pallas_call(
@@ -514,10 +541,12 @@
             jax.ShapeDtypeStruct((5, PZ, PX, PY), f32),
             jax.ShapeDtypeStruct((3, PX, PY), f32),
         ),
-        in_specs=[any_space, any_space, any_space, vmem, vmem],
+        in_specs=[any_space] * 5,
         out_specs=(any_space, any_space),
         scratch_shapes=[
             pltpu.VMEM((5, PZ, PX, PY), f32),
+            pltpu.VMEM((4, 2 * PY), f32),
+            pltpu.VMEM((8, 2 * PY), jnp.int32),
             pltpu.VMEM(padded, f32),
             pltpu.VMEM(padded, f32),
             pltpu.VMEM(padded, f32),
@@ -536,13 +565,13 @@
             pltpu.VMEM((5, PZ, PX, PY), f32),
             pltpu.VMEM((4, PZ, PX, PY), f32),
             pltpu.VMEM((PZ, PX, PY), jnp.int32),
-            pltpu.VMEM((12, 8, PY), f32),
+            pltpu.VMEM((6, 8, PY), jnp.int32),
             pltpu.VMEM((8, 4, PX, PY), f32),
             pltpu.VMEM((4, 4, PX, PY), f32),
             pltpu.VMEM((4, 4, PX, PY), f32),
             pltpu.VMEM((4, 4, PX, PY), f32),
             pltpu.VMEM((3, PX, PY), f32),
-            dma((3,)),
+            dma((5,)),
             dma((2,)),
             dma((3, 6)),
             dma((3, 6)),
@@ -550,13 +579,14 @@
             dma((ND - 1,)),
             dma((len(PAIRS),)),
             dma((len(PAIRS),)),
+            pltpu.SemaphoreType.REGULAR,
             dma((4,)),
             dma((4,)),
             dma((4,)),
             dma((4,)),
         ],
         compiler_params=pltpu.CompilerParams(
-            collective_id=0, has_side_effects=True, vmem_limit_bytes=40 * 1024 * 1024
+            collective_id=0, has_side_effects=True, vmem_limit_bytes=60 * 1024 * 1024
         ),
     )(density, velocity, pressure, palette, palette_index)
     return fluid_state, picture[None]

time: 53.5 us -> 45.3 us (0.85)
  Pallas kernels: 46.7 us -> 41.5 us
  local copies, waits for them, and re-layouts: 5.87 us -> 2.91 us
    pallas_call x1, Pallas kernels: 46.7 us -> 41.5 us  [shards(): pl.pallas_call(kernel, out_shape=(jax.ShapeDtypeStruct((5, PZ, PX, PY), f...]
    unnamed x12 -> x4, local copies, waits for them, and re-layouts: 5.87 us -> 2.91 us
where the time goes in v2:
time: 45.3 us; the launch traced here: 45.1 us
  Pallas kernels  41.5 us (92%)
  local copies, waits for them, and re-layouts  2.91 us (6%)
  between operations  0.65 us (1%)
    pallas_call x1, Pallas kernels, shards(): pl.pallas_call(kernel, out_shape=(jax.ShapeDtypeStruct((5, PZ, PX, PY), f...  41.5 us
    unnamed x4, local copies, waits for them, and re-layouts  2.91 us

profile of v2, /device:TPU:1, one launch (start us, length us, event | category | flops | bytes accessed | tf_op | source)
XLA Modules:
  0.0 45.1 jit_solution(16079926314939799831)
XLA Ops:
  0.6 41.5 %shard_map.68 = (f32[5,8,48,128]{3,2,1,0:T(8,128)}, f32[3,48,128]{2,1,0:T(8,128)}) custom-call(f32[8,48,128]{2,1,0:T(8,128)} %density_in.1, f32[3,8,48,128]{3,2,1,0:T(8,128)} %velocity_in.1, f32[8,48,128]{2,1,0:T(8,128)} %pressure_in.1, f32[4,256]{1,0:T(4,128)} %palette_in.1, s32[8,256]{1,0:T(8,128)} %index_in.1), custom_call_target="tpu_custom_call" | custom-call | tf_op jit(solution)/shard_map/pallas_call | solution.py:538
  42.2 0.0 copy-start
  42.2 2.3 %copy.9 = f32[5,8,48,128]{3,2,1,0:T(8,128)} copy(f32[5,8,48,128]{3,2,1,0:T(8,128)} %get-tuple-element.8) | data formatting | bytes 1966080
  44.5 0.0 copy-done
  44.5 0.6 %copy.10 = f32[1,3,48,128]{3,2,1,0:T(8,128)} copy(f32[1,3,48,128]{3,2,1,0:T(8,128)S(1)} %bitcast.1) | data formatting | bytes 147456
Async XLA Ops:
  42.2 2.3 %copy-start = (f32[3,48,128]{2,1,0:T(8,128)S(1)}, f32[3,48,128]{2,1,0:T(8,128)}, u32[]{:S(2)}) copy-start(f32[3,48,128]{2,1,0:T(8,128)} %get-tuple-element.5) | copy-start | bytes 221188

commit v3 on v2

--- a/solution.py
+++ b/solution.py
@@ -55,6 +55,7 @@
     x_recv,
     y_send,
     y_recv,
+    x_part,
     y_part,
     max_own,
     max_line,
@@ -163,20 +164,30 @@
             for k, (src, dst, device) in enumerate(plan)
         ]
 
-    def receive(s, copies):
-        state, derived = states[s], prims[s]
+    row_of = lax.broadcasted_iota(jnp.int32, (8, PY), 0)
+    at_top, at_bottom = row_of == 0, row_of == 7
+
+    def from_outside(inner, outer, component, sign):
+        prim_in, prim_out = primitives(inner), primitives(outer)
+        fastest = jnp.maximum(
+            jnp.abs(prim_in[component - 1]) + prim_in[4],
+            jnp.abs(prim_out[component - 1]) + prim_out[4],
+        )
+        flows = flux(outer, prim_out[component - 1], prim_out[3], component)
+        return [sign(flows[c]) + fastest * (outer[c] - inner[c]) for c in range(5)]
+
+    def receive_sides(s, copies):
         copies[4].wait_recv()
         copies[5].wait_recv()
-        for side, wall, row in ((0, g == 0, TOP - 1), (1, g == NG - 1, TOP + PX)):
-            cells = []
+        for side, wall in ((0, g == 0), (1, g == NG - 1)):
+            own = [x_send[s, side, c] for c in range(5)]
+            near = [
+                jnp.where(wall, -own[c] if c == 1 else own[c], x_recv[s, side, c])
+                for c in range(5)
+            ]
+            parts = from_outside(own, near, 1, (lambda f: f) if side == 0 else (lambda f: -f))
             for c in range(5):
-                own = x_send[s, side, c]
-                cells.append(jnp.where(wall, -own if c == 1 else own, x_recv[s, side, c]))
-            values = primitives(cells)
-            for c in range(5):
-                for z in range(PZ):
-                    state[c, z + 1, row : row + 1, :] = cells[c][z : z + 1]
-                    derived[c, z + 1, row : row + 1, :] = values[c][z : z + 1]
+                x_part[side, c] = parts[c]
         copies[2].wait_recv()
         copies[3].wait_recv()
 
@@ -193,18 +204,15 @@
                         pltpu.roll(right, (PY - 1 - 16 * c) % PY, 1),
                     )
                 )
-            prim_in, prim_out = primitives(inner), primitives(outer)
-            fastest = jnp.maximum(
-                jnp.abs(prim_in[1]) + prim_in[4], jnp.abs(prim_out[1]) + prim_out[4]
-            )
-            flows = flux(outer, prim_out[1], prim_out[3], 2)
+            parts = from_outside(inner, outer, 2, lambda f: jnp.where(even, f, -f))
             for c in range(5):
-                y_part[c, rows, :] = jnp.where(even, flows[c], -flows[c]) + fastest * (
-                    outer[c] - inner[c]
-                )
+                y_part[c, rows, :] = parts[c]
             return carry
 
-        lax.fori_loop(0, NB, edge, 0)
+        lax.fori_loop(0, NB, edge, 0, unroll=2)
+
+    def receive_planes(s, copies):
+        state, derived = states[s], prims[s]
         copies[0].wait_recv()
         copies[1].wait_recv()
 
@@ -216,42 +224,103 @@
                     derived[c, z, rows, :] = values[c]
             return carry
 
-        lax.fori_loop(0, NB, plane, 0)
-
-    def twice_tendency(s, z, r):
+        lax.fori_loop(0, NB, plane, 0, unroll=2)
+
+    def add(total, parts):
+        return parts if total is None else [t + p for t, p in zip(total, parts)]
+
+    def along_z(s, z, row, cell, prim, total):
+        state, derived = states[s], prims[s]
+        here = jnp.abs(prim[2]) + prim[4]
+        for side in (-1, 1):
+            zz = z + 1 + side
+            near = [state[c, zz, row : row + 8, :] for c in range(5)]
+            q, p = derived[2, zz, row : row + 8, :], derived[3, zz, row : row + 8, :]
+            fastest = jnp.maximum(here, jnp.abs(q) + derived[4, zz, row : row + 8, :])
+            flows = flux(near, q, p, 3)
+            parts = [fastest * (near[c] - cell[c]) for c in range(5)]
+            parts = [a + f if side < 0 else a - f for a, f in zip(parts, flows)]
+            total = add(total, parts)
+        return total
+
+    def centre(s, z, row):
+        cell = [states[s][c, z + 1, row : row + 8, :] for c in range(5)]
+        return cell, [prims[s][c, z + 1, row : row + 8, :] for c in range(5)]
+
+    def within(s, z, r, with_z):
         state, derived = states[s], prims[s]
         row = TOP + 8 * r
-        cell = [state[c, z + 1, row : row + 8, :] for c in range(5)]
-        prim = [derived[c, z + 1, row : row + 8, :] for c in range(5)]
-        total = [None] * 5
-        for axis, component in ((0, 3), (1, 1)):
-            here = jnp.abs(prim[component - 1]) + prim[4]
-            for side in (-1, 1):
-                zz = z + 1 + (side if axis == 0 else 0)
-                rr = row + (side if axis == 1 else 0)
-                near = [state[c, zz, rr : rr + 8, :] for c in range(5)]
-                q = derived[component - 1, zz, rr : rr + 8, :]
-                p = derived[3, zz, rr : rr + 8, :]
-                fastest = jnp.maximum(here, jnp.abs(q) + derived[4, zz, rr : rr + 8, :])
-                flows = flux(near, q, p, component)
-                for c in range(5):
-                    part = fastest * (near[c] - cell[c])
-                    part = part + flows[c] if side < 0 else part - flows[c]
-                    total[c] = part if total[c] is None else total[c] + part
+        cell, prim = centre(s, z, row)
+        total = along_z(s, z, row, cell, prim, None) if with_z else None
+        here = jnp.abs(prim[0]) + prim[4]
+        for side in (-1, 1):
+            rr = row + side
+            near = [state[c, z + 1, rr : rr + 8, :] for c in range(5)]
+            q, p = derived[0, z + 1, rr : rr + 8, :], derived[3, z + 1, rr : rr + 8, :]
+            fastest = jnp.maximum(here, jnp.abs(q) + derived[4, z + 1, rr : rr + 8, :])
+            flows = flux(near, q, p, 1)
+            parts = [fastest * (near[c] - cell[c]) for c in range(5)]
+            parts = [a + f if side < 0 else a - f for a, f in zip(parts, flows)]
+            if side < 0 and r == 0:
+                parts = [jnp.where(at_top, 0.0, a) for a in parts]
+            if side > 0 and r == NB - 1:
+                parts = [jnp.where(at_bottom, 0.0, a) for a in parts]
+            total = add(total, parts)
         here = jnp.abs(prim[1]) + prim[4]
-        turn = lax.rem(PY - 2 * z, PY)
-        edges = [pltpu.roll(y_part[c, 8 * r : 8 * r + 8, :], turn, 1) for c in range(5)]
         for side in (-1, 1):
             shift = 1 if side < 0 else PY - 1
             near = [pltpu.roll(cell[c], shift, 1) for c in range(5)]
             q, p = pltpu.roll(prim[1], shift, 1), pltpu.roll(prim[3], shift, 1)
             fastest = jnp.maximum(here, pltpu.roll(here, shift, 1))
             flows = flux(near, q, p, 2)
+            parts = [fastest * (near[c] - cell[c]) for c in range(5)]
+            parts = [a + f if side < 0 else a - f for a, f in zip(parts, flows)]
+            outside = at_first if side < 0 else at_last
+            total = add(total, [jnp.where(outside, 0.0, a) for a in parts])
+        return total
+
+    def completed(s, z, r, with_z):
+        rows = slice(8 * r, 8 * r + 8)
+        total = [tend[c, z, rows, :] for c in range(5)]
+        turn = lax.rem(PY - 2 * z, PY)
+        for c in range(5):
+            edges = pltpu.roll(y_part[c, rows, :], turn, 1)
+            total[c] = total[c] + jnp.where(at_first | at_last, edges, 0.0)
+        for side, block, place in ((0, 0, at_top), (1, NB - 1, at_bottom)):
+            if r == block:
+                for c in range(5):
+                    line = jnp.broadcast_to(x_part[side, c, pl.ds(z, 1), :], (8, PY))
+                    total[c] = total[c] + jnp.where(place, line, 0.0)
+        if with_z:
+            row = TOP + 8 * r
+            cell, prim = centre(s, z, row)
+            total = along_z(s, z, row, cell, prim, total)
+        return total
+
+    def middle_planes(visit):
+        def one(z, carry):
+            for r in range(NB):
+                visit(z, r, False)
+            return carry
+
+        lax.fori_loop(1, PZ - 1, one, 0)
+
+    def end_planes(visit):
+        def one(k, carry):
+            for r in range(NB):
+                visit((PZ - 1) * k, r, True)
+            return carry
+
+        lax.fori_loop(0, 2, one, 0)
+
+    def inside(s):
+        def visit(z, r, at_end):
+            total = within(s, z, r, not at_end)
             for c in range(5):
-                part = fastest * (near[c] - cell[c])
-                part = part + flows[c] if side < 0 else part - flows[c]
-                total[c] = total[c] + jnp.where(at_first if side < 0 else at_last, edges[c], part)
-        return total
+                tend[c, z, 8 * r : 8 * r + 8, :] = total[c]
+
+        middle_planes(visit)
+        end_planes(visit)
 
     for load in loads[:3]:
         load.wait()
@@ -323,8 +392,8 @@
         pal_high = jnp.broadcast_to(palette_ref[c : c + 1, PY : 2 * PY], (8, PY))
         levels = []
         for b in bins:
-            within = b & (PY - 1)
-            colour = jnp.where(b < PY, take(pal_low, within), take(pal_high, within))
+            spot = b & (PY - 1)
+            colour = jnp.where(b < PY, take(pal_low, spot), take(pal_high, spot))
             levels.append((colour * (1.0 / STEP) + 0.5).astype(jnp.int32))
         levels.append(pltpu.roll(levels[0], PY - 1, 1))
         words.append(levels)
@@ -332,17 +401,17 @@
         for c in range(2):
             tables[2 * k + c] = (words[c][k] - 32768) * 65536 + words[c + 2][k]
 
-    receive(0, halos[0])
-
-    def tend_plane(z, carry):
-        for r in range(NB):
-            total = twice_tendency(0, z, r)
-            for c in range(5):
-                tend[c, z, 8 * r : 8 * r + 8, :] = total[c]
-        return carry
-
-    lax.fori_loop(0, PZ, tend_plane, 0)
-
+    inside(0)
+    receive_sides(0, halos[0])
+    receive_planes(0, halos[0])
+
+    def complete(z, r, at_end):
+        total = completed(0, z, r, at_end)
+        for c in range(5):
+            tend[c, z, 8 * r : 8 * r + 8, :] = total[c]
+
+    middle_planes(complete)
+    end_planes(complete)
     for copy in planes:
         copy.wait_recv()
     most = max_mid[...]
@@ -352,65 +421,67 @@
         jnp.max(most, axis=(0, 1), keepdims=True), (8, PY)
     )
 
-    def section_one(z, carry):
-        for r in range(NB):
-            new = [
-                u_first[c, z + 1, TOP + 8 * r : TOP + 8 * r + 8, :]
-                + half_step * tend[c, z, 8 * r : 8 * r + 8, :]
-                for c in range(5)
-            ]
-            put(1, z, r, new, primitives(new))
-        return carry
-
-    lax.fori_loop(0, PZ, section_one, 0)
+    def section_one(z, r, at_end):
+        row = TOP + 8 * r
+        new = [
+            u_first[c, z + 1, row : row + 8, :]
+            + half_step * tend[c, z, 8 * r : 8 * r + 8, :]
+            for c in range(5)
+        ]
+        put(1, z, r, new, primitives(new))
+
+    def section_two(z, r, at_end):
+        total = completed(1, z, r, at_end)
+        row = TOP + 8 * r
+        new = [
+            0.75 * u_first[c, z + 1, row : row + 8, :]
+            + 0.25 * (u_second[c, z + 1, row : row + 8, :] + half_step * total[c])
+            for c in range(5)
+        ]
+        put(2, z, r, new, primitives(new))
+
+    def section_three(z, r, at_end):
+        total = completed(2, z, r, at_end)
+        row = TOP + 8 * r
+        rows = slice(8 * r, 8 * r + 8)
+        new = [
+            u_first[c, z + 1, row : row + 8, :] * (1.0 / 3.0)
+            + (2.0 / 3.0) * (u_third[c, z + 1, row : row + 8, :] + half_step * total[c])
+            for c in range(5)
+        ]
+        for c in range(5):
+            fluid[c, z, rows, :] = new[c]
+        inverse = 1.0 / new[0]
+        kinetic = 0.5 * inverse * (new[1] * new[1] + new[2] * new[2] + new[3] * new[3])
+        position = jnp.clip(new[0] - 0.5, 0.0, 1.0) * 255.0
+        index = (position * 0.5).astype(jnp.int32)
+        past = position - 2.0 * index.astype(jnp.float32)
+        shade_index[z, rows, :] = index
+        shade[0, z, rows, :] = 1.0 - jnp.minimum(past, 1.0)
+        shade[1, z, rows, :] = jnp.maximum(past - 1.0, 0.0)
+        shade[2, z, rows, :] = new[0] * (-2.0 * STEP / (PZ * ND))
+        shade[3, z, rows, :] = (STEP * (HEAT_RATIO - 1.0)) * (new[4] - kinetic) * inverse
+
     halos.append(halo(1))
-    for copy in halos[1]:
+    end_planes(section_one)
+    for copy in halos[1][:2]:
         copy.start()
-    receive(1, halos[1])
-
-    def section_two(z, carry):
-        for r in range(NB):
-            total = twice_tendency(1, z, r)
-            row = TOP + 8 * r
-            new = [
-                0.75 * u_first[c, z + 1, row : row + 8, :]
-                + 0.25 * (u_second[c, z + 1, row : row + 8, :] + half_step * total[c])
-                for c in range(5)
-            ]
-            put(2, z, r, new, primitives(new))
-        return carry
-
-    lax.fori_loop(0, PZ, section_two, 0)
+    middle_planes(section_one)
+    for copy in halos[1][2:]:
+        copy.start()
+    inside(1)
+    receive_sides(1, halos[1])
+    middle_planes(section_two)
+    receive_planes(1, halos[1])
     halos.append(halo(2))
+    end_planes(section_two)
     for copy in halos[2]:
         copy.start()
-    receive(2, halos[2])
-
-    def section_three(z, carry):
-        for r in range(NB):
-            total = twice_tendency(2, z, r)
-            row = TOP + 8 * r
-            rows = slice(8 * r, 8 * r + 8)
-            new = [
-                u_first[c, z + 1, row : row + 8, :] * (1.0 / 3.0)
-                + (2.0 / 3.0) * (u_third[c, z + 1, row : row + 8, :] + half_step * total[c])
-                for c in range(5)
-            ]
-            for c in range(5):
-                fluid[c, z, rows, :] = new[c]
-            inverse = 1.0 / new[0]
-            kinetic = 0.5 * inverse * (new[1] * new[1] + new[2] * new[2] + new[3] * new[3])
-            position = jnp.clip(new[0] - 0.5, 0.0, 1.0) * 255.0
-            index = (position * 0.5).astype(jnp.int32)
-            past = position - 2.0 * index.astype(jnp.float32)
-            shade_index[z, rows, :] = index
-            shade[0, z, rows, :] = 1.0 - jnp.minimum(past, 1.0)
-            shade[1, z, rows, :] = jnp.maximum(past - 1.0, 0.0)
-            shade[2, z, rows, :] = new[0] * (-2.0 * STEP / (PZ * ND))
-            shade[3, z, rows, :] = (STEP * (HEAT_RATIO - 1.0)) * (new[4] - kinetic) * inverse
-        return carry
-
-    lax.fori_loop(0, PZ, section_three, 0)
+    inside(2)
+    receive_sides(2, halos[2])
+    middle_planes(section_three)
+    receive_planes(2, halos[2])
+    end_planes(section_three)
     fluid_store = pltpu.make_async_copy(fluid, fluid_out, store_sem.at[0])
     fluid_store.start()
 
@@ -557,6 +628,7 @@
             pltpu.VMEM((3, 2, 5, PZ, PY), f32),
             pltpu.VMEM((3, PX, PY), f32),
             pltpu.VMEM((3, 2, PX, PY), f32),
+            pltpu.VMEM((2, 5, PZ, PY), f32),
             pltpu.VMEM((5, PX, PY), f32),
             pltpu.VMEM((8, PY), f32),
             pltpu.VMEM((ND - 1, 8, PY), f32),

time: 45.3 us -> 41.5 us (0.916)
  Pallas kernels: 41.5 us -> 37.8 us
    pallas_call x1, Pallas kernels: 41.5 us -> 37.8 us  [shards(): pl.pallas_call(kernel, out_shape=(jax.ShapeDtypeStruct((5, PZ, PX, PY), f...]
where the time goes in v3:
time: 41.5 us; the launch traced here: 41.4 us
  Pallas kernels  37.8 us (91%)
  local copies, waits for them, and re-layouts  2.91 us (7%)
  between operations  0.65 us (2%)
    pallas_call x1, Pallas kernels, shards(): pl.pallas_call(kernel, out_shape=(jax.ShapeDtypeStruct((5, PZ, PX, PY), f...  37.8 us
    unnamed x4, local copies, waits for them, and re-layouts  2.91 us

profile of v3, /device:TPU:1, one launch (start us, length us, event | category | flops | bytes accessed | tf_op | source)
XLA Modules:
  0.0 41.4 jit_solution(16279458167935217068)
XLA Ops:
  0.6 37.8 %shard_map.68 = (f32[5,8,48,128]{3,2,1,0:T(8,128)}, f32[3,48,128]{2,1,0:T(8,128)}) custom-call(f32[8,48,128]{2,1,0:T(8,128)} %density_in.1, f32[3,8,48,128]{3,2,1,0:T(8,128)} %velocity_in.1, f32[8,48,128]{2,1,0:T(8,128)} %pressure_in.1, f32[4,256]{1,0:T(4,128)} %palette_in.1, s32[8,256]{1,0:T(8,128)} %index_in.1), custom_call_target="tpu_custom_call" | custom-call | tf_op jit(solution)/shard_map/pallas_call | solution.py:609
  38.4 0.0 copy-start
  38.5 2.3 %copy.9 = f32[5,8,48,128]{3,2,1,0:T(8,128)} copy(f32[5,8,48,128]{3,2,1,0:T(8,128)} %get-tuple-element.8) | data formatting | bytes 1966080
  40.7 0.0 copy-done
  40.7 0.6 %copy.10 = f32[1,3,48,128]{3,2,1,0:T(8,128)} copy(f32[1,3,48,128]{3,2,1,0:T(8,128)S(1)} %bitcast.1) | data formatting | bytes 147456
Async XLA Ops:
  38.4 2.3 %copy-start = (f32[3,48,128]{2,1,0:T(8,128)S(1)}, f32[3,48,128]{2,1,0:T(8,128)}, u32[]{:S(2)}) copy-start(f32[3,48,128]{2,1,0:T(8,128)} %get-tuple-element.5) | copy-start | bytes 221188

commit v4 on v3

--- a/solution.py
+++ b/solution.py
@@ -51,6 +51,7 @@
     prim_a,
     prim_b,
     tend,
+    tend_recv,
     x_send,
     x_recv,
     y_send,
@@ -136,17 +137,23 @@
         for c in range(5):
             states[s][c, z + 1, rows, :] = new[c]
             prims[s][c, z + 1, rows, :] = derived[c]
-        pack_edges(s, z, r, new)
+        pack_edges(3 if s == 1 else s, z, r, new)
 
     def halo(s):
         up_d, down_d = lax.rem(d + 1, ND), lax.rem(d + ND - 1, ND)
         up_g, down_g = lax.rem(g + 1, NG), lax.rem(g + NG - 1, NG)
         up_i, down_i = lax.rem(i + 1, NI), lax.rem(i + NI - 1, NI)
         rows = pl.ds(TOP, PX)
-        state = states[s]
+        if s == 1:
+            below, above = tend.at[:, 0], tend.at[:, PZ - 1]
+            to_above, to_below = tend_recv.at[1], tend_recv.at[0]
+        else:
+            state = states[s]
+            below, above = state.at[:, 1, rows, :], state.at[:, PZ, rows, :]
+            to_above, to_below = state.at[:, PZ + 1, rows, :], state.at[:, 0, rows, :]
         plan = [
-            (state.at[:, 1, rows, :], state.at[:, PZ + 1, rows, :], {"depth": down_d}),
-            (state.at[:, PZ, rows, :], state.at[:, 0, rows, :], {"depth": up_d}),
+            (below, to_above, {"depth": down_d}),
+            (above, to_below, {"depth": up_d}),
             (y_send.at[s], y_recv.at[s, 1], {"image": down_i}),
             (y_send.at[s], y_recv.at[s, 0], {"image": up_i}),
             (x_send.at[s, 0], x_recv.at[s, 1], {"group": down_g}),
@@ -177,8 +184,10 @@
         return [sign(flows[c]) + fastest * (outer[c] - inner[c]) for c in range(5)]
 
     def receive_sides(s, copies):
-        copies[4].wait_recv()
-        copies[5].wait_recv()
+        s = 3 if s == 1 else s
+        if copies is not None:
+            copies[4].wait_recv()
+            copies[5].wait_recv()
         for side, wall in ((0, g == 0), (1, g == NG - 1)):
             own = [x_send[s, side, c] for c in range(5)]
             near = [
@@ -188,8 +197,9 @@
             parts = from_outside(own, near, 1, (lambda f: f) if side == 0 else (lambda f: -f))
             for c in range(5):
                 x_part[side, c] = parts[c]
-        copies[2].wait_recv()
-        copies[3].wait_recv()
+        if copies is not None:
+            copies[2].wait_recv()
+            copies[3].wait_recv()
 
         def edge(r, carry):
             rows = pl.ds(pl.multiple_of(8 * r, 8), 8)
@@ -213,8 +223,9 @@
 
     def receive_planes(s, copies):
         state, derived = states[s], prims[s]
-        copies[0].wait_recv()
-        copies[1].wait_recv()
+        if copies is not None:
+            copies[0].wait_recv()
+            copies[1].wait_recv()
 
         def plane(r, carry):
             rows = pl.ds(pl.multiple_of(TOP + 8 * r, 8), 8)
@@ -279,9 +290,10 @@
             total = add(total, [jnp.where(outside, 0.0, a) for a in parts])
         return total
 
-    def completed(s, z, r, with_z):
+    def completed(s, z, r, with_z, total=None):
         rows = slice(8 * r, 8 * r + 8)
-        total = [tend[c, z, rows, :] for c in range(5)]
+        if total is None:
+            total = [tend[c, z, rows, :] for c in range(5)]
         turn = lax.rem(PY - 2 * z, PY)
         for c in range(5):
             edges = pltpu.roll(y_part[c, rows, :], turn, 1)
@@ -325,16 +337,24 @@
     for load in loads[:3]:
         load.wait()
 
-    def first(z, most):
+    def signals(z, most):
+        for r in range(NB):
+            rho, u, v, w, p = [raw[c, z, 8 * r : 8 * r + 8, :] for c in range(5)]
+            sound = jnp.sqrt(HEAT_RATIO * p / rho)
+            prims[0][4, z + 1, TOP + 8 * r : TOP + 8 * r + 8, :] = sound
+            most = jnp.maximum(most, jnp.abs(u) + jnp.abs(v) + jnp.abs(w) + 3.0 * sound)
+        return most
+
+    max_own[...] = lax.fori_loop(0, PZ, signals, jnp.zeros((8, PY), jnp.float32), unroll=2)
+
+    def first(z, carry):
         for r in range(NB):
             rho, u, v, w, p = [raw[c, z, 8 * r : 8 * r + 8, :] for c in range(5)]
             energy = p / (HEAT_RATIO - 1.0) + 0.5 * rho * (u * u + v * v + w * w)
-            sound = jnp.sqrt(HEAT_RATIO * p / rho)
+            sound = prims[0][4, z + 1, TOP + 8 * r : TOP + 8 * r + 8, :]
             put(0, z, r, [rho, rho * u, rho * v, rho * w, energy], [u, v, w, p, sound])
-            most = jnp.maximum(most, jnp.abs(u) + jnp.abs(v) + jnp.abs(w) + 3.0 * sound)
-        return most
-
-    max_own[...] = lax.fori_loop(0, PZ, first, jnp.zeros((8, PY), jnp.float32))
+        return carry
+
     pl.semaphore_wait(barrier, ND + NG + NI - 3)
 
     for o in range(1, NI):
@@ -354,9 +374,11 @@
     ]
     for copy in lines:
         copy.start()
+    lax.fori_loop(0, PZ, first, 0)
     halos = [halo(0)]
     for copy in halos[0]:
         copy.start()
+    inside(0)
     for copy in lines:
         copy.wait_recv()
     most = max_own[...]
@@ -401,7 +423,6 @@
         for c in range(2):
             tables[2 * k + c] = (words[c][k] - 32768) * 65536 + words[c + 2][k]
 
-    inside(0)
     receive_sides(0, halos[0])
     receive_planes(0, halos[0])
 
@@ -409,9 +430,13 @@
         total = completed(0, z, r, at_end)
         for c in range(5):
             tend[c, z, 8 * r : 8 * r + 8, :] = total[c]
+        pack_edges(1, z, r, total)
 
     middle_planes(complete)
     end_planes(complete)
+    halos.append(halo(1))
+    for copy in halos[1]:
+        copy.start()
     for copy in planes:
         copy.wait_recv()
     most = max_mid[...]
@@ -431,7 +456,7 @@
         put(1, z, r, new, primitives(new))
 
     def section_two(z, r, at_end):
-        total = completed(1, z, r, at_end)
+        total = completed(1, z, r, False, within(1, z, r, True))
         row = TOP + 8 * r
         new = [
             0.75 * u_first[c, z + 1, row : row + 8, :]
@@ -462,21 +487,41 @@
         shade[2, z, rows, :] = new[0] * (-2.0 * STEP / (PZ * ND))
         shade[3, z, rows, :] = (STEP * (HEAT_RATIO - 1.0)) * (new[4] - kinetic) * inverse
 
-    halos.append(halo(1))
+    middle_planes(section_one)
     end_planes(section_one)
-    for copy in halos[1][:2]:
-        copy.start()
-    middle_planes(section_one)
-    for copy in halos[1][2:]:
-        copy.start()
-    inside(1)
-    receive_sides(1, halos[1])
-    middle_planes(section_two)
-    receive_planes(1, halos[1])
+    for copy in halos[1]:
+        copy.wait_recv()
+    for side in range(2):
+        for c in range(5):
+            x_recv[3, side, c] = x_recv[0, side, c] + half_step * x_recv[1, side, c]
+        for r in range(NB):
+            rows = slice(8 * r, 8 * r + 8)
+            y_recv[3, side, rows, :] = (
+                y_recv[0, side, rows, :] + half_step * y_recv[1, side, rows, :]
+            )
+
+    def outer_planes(r, carry):
+        rows = pl.ds(pl.multiple_of(8 * r, 8), 8)
+        padded = pl.ds(pl.multiple_of(TOP + 8 * r, 8), 8)
+        for side, z in ((0, 0), (1, PZ + 1)):
+            for c in range(5):
+                u_second[c, z, padded, :] = (
+                    u_first[c, z, padded, :] + half_step * tend_recv[side, c, rows, :]
+                )
+        return carry
+
+    lax.fori_loop(0, NB, outer_planes, 0, unroll=2)
+    receive_sides(1, None)
+    receive_planes(1, None)
     halos.append(halo(2))
     end_planes(section_two)
-    for copy in halos[2]:
+    for copy in halos[2][:2]:
         copy.start()
+    middle_planes(section_two)
+    for copy in halos[2][2:]:
+        copy.start()
+    for copy in halos[1]:
+        copy.wait_send()
     inside(2)
     receive_sides(2, halos[2])
     middle_planes(section_three)
@@ -590,7 +635,7 @@
     picture_store = pltpu.make_async_copy(picture, picture_out, store_sem.at[1])
     picture_store.start()
 
-    for copy in lines + planes + halos[0] + halos[1] + halos[2]:
+    for copy in lines + planes + halos[0] + halos[2]:
         copy.wait_send()
     for k in range(4):
         pair_copy(k).wait_send()
@@ -624,10 +669,11 @@
             pltpu.VMEM(padded, f32),
             pltpu.VMEM(padded, f32),
             pltpu.VMEM((5, PZ, PX, PY), f32),
-            pltpu.VMEM((3, 2, 5, PZ, PY), f32),
-            pltpu.VMEM((3, 2, 5, PZ, PY), f32),
-            pltpu.VMEM((3, PX, PY), f32),
-            pltpu.VMEM((3, 2, PX, PY), f32),
+            pltpu.VMEM((2, 5, PX, PY), f32),
+            pltpu.VMEM((4, 2, 5, PZ, PY), f32),
+            pltpu.VMEM((4, 2, 5, PZ, PY), f32),
+            pltpu.VMEM((4, PX, PY), f32),
+            pltpu.VMEM((4, 2, PX, PY), f32),
             pltpu.VMEM((2, 5, PZ, PY), f32),
             pltpu.VMEM((5, PX, PY), f32),
             pltpu.VMEM((8, PY), f32),

time: 41.5 us -> 40.2 us (0.969)
  Pallas kernels: 37.8 us -> 36.5 us
    pallas_call x1, Pallas kernels: 37.8 us -> 36.5 us  [shards(): pl.pallas_call(kernel, out_shape=(jax.ShapeDtypeStruct((5, PZ, PX, PY), f...]
where the time goes in v4:
time: 40.2 us; the launch traced here: 40.1 us
  Pallas kernels  36.5 us (91%)
  local copies, waits for them, and re-layouts  2.91 us (7%)
  between operations  0.65 us (2%)
    pallas_call x1, Pallas kernels, shards(): pl.pallas_call(kernel, out_shape=(jax.ShapeDtypeStruct((5, PZ, PX, PY), f...  36.5 us
    unnamed x4, local copies, waits for them, and re-layouts  2.91 us

profile of v4, /device:TPU:1, one launch (start us, length us, event | category | flops | bytes accessed | tf_op | source)
XLA Modules:
  0.0 40.1 jit_solution(366764553576568794)
XLA Ops:
  0.6 36.5 %shard_map.68 = (f32[5,8,48,128]{3,2,1,0:T(8,128)}, f32[3,48,128]{2,1,0:T(8,128)}) custom-call(f32[8,48,128]{2,1,0:T(8,128)} %density_in.1, f32[3,8,48,128]{3,2,1,0:T(8,128)} %velocity_in.1, f32[8,48,128]{2,1,0:T(8,128)} %pressure_in.1, f32[4,256]{1,0:T(4,128)} %palette_in.1, s32[8,256]{1,0:T(8,128)} %index_in.1), custom_call_target="tpu_custom_call" | custom-call | tf_op jit(solution)/shard_map/pallas_call | solution.py:654
  37.2 0.0 copy-start
  37.2 2.3 %copy.9 = f32[5,8,48,128]{3,2,1,0:T(8,128)} copy(f32[5,8,48,128]{3,2,1,0:T(8,128)} %get-tuple-element.8) | data formatting | bytes 1966080
  39.4 0.0 copy-done
  39.4 0.6 %copy.10 = f32[1,3,48,128]{3,2,1,0:T(8,128)} copy(f32[1,3,48,128]{3,2,1,0:T(8,128)S(1)} %bitcast.1) | data formatting | bytes 147456
Async XLA Ops:
  37.2 2.3 %copy-start = (f32[3,48,128]{2,1,0:T(8,128)S(1)}, f32[3,48,128]{2,1,0:T(8,128)}, u32[]{:S(2)}) copy-start(f32[3,48,128]{2,1,0:T(8,128)} %get-tuple-element.5) | copy-start | bytes 221188

commit v5 on v4

--- a/solution.py
+++ b/solution.py
@@ -317,6 +317,14 @@
 
         lax.fori_loop(1, PZ - 1, one, 0)
 
+    def all_planes(visit):
+        def one(z, carry):
+            for r in range(NB):
+                visit(z, r, False)
+            return carry
+
+        lax.fori_loop(0, PZ, one, 0, unroll=2)
+
     def end_planes(visit):
         def one(k, carry):
             for r in range(NB):
@@ -400,6 +408,23 @@
     for copy in planes:
         copy.start()
 
+    receive_sides(0, halos[0])
+    receive_planes(0, halos[0])
+
+    def complete(z, r, at_end):
+        total = completed(0, z, r, at_end)
+        for c in range(5):
+            tend[c, z, 8 * r : 8 * r + 8, :] = total[c]
+        pack_edges(1, z, r, total)
+
+    halos.append(halo(1))
+    end_planes(complete)
+    for copy in halos[1][:2]:
+        copy.start()
+    middle_planes(complete)
+    for copy in halos[1][2:]:
+        copy.start()
+
     for load in loads[3:]:
         load.wait()
     pick = lax.rem(2 * lane, PY)
@@ -422,21 +447,6 @@
     for k in range(3):
         for c in range(2):
             tables[2 * k + c] = (words[c][k] - 32768) * 65536 + words[c + 2][k]
-
-    receive_sides(0, halos[0])
-    receive_planes(0, halos[0])
-
-    def complete(z, r, at_end):
-        total = completed(0, z, r, at_end)
-        for c in range(5):
-            tend[c, z, 8 * r : 8 * r + 8, :] = total[c]
-        pack_edges(1, z, r, total)
-
-    middle_planes(complete)
-    end_planes(complete)
-    halos.append(halo(1))
-    for copy in halos[1]:
-        copy.start()
     for copy in planes:
         copy.wait_recv()
     most = max_mid[...]
@@ -466,7 +476,7 @@
         put(2, z, r, new, primitives(new))
 
     def section_three(z, r, at_end):
-        total = completed(2, z, r, at_end)
+        total = completed(2, z, r, False)
         row = TOP + 8 * r
         rows = slice(8 * r, 8 * r + 8)
         new = [
@@ -487,8 +497,7 @@
         shade[2, z, rows, :] = new[0] * (-2.0 * STEP / (PZ * ND))
         shade[3, z, rows, :] = (STEP * (HEAT_RATIO - 1.0)) * (new[4] - kinetic) * inverse
 
-    middle_planes(section_one)
-    end_planes(section_one)
+    all_planes(section_one)
     for copy in halos[1]:
         copy.wait_recv()
     for side in range(2):
@@ -523,10 +532,17 @@
     for copy in halos[1]:
         copy.wait_send()
     inside(2)
+    receive_planes(2, halos[2])
+
+    def with_planes(z, r, at_end):
+        row = TOP + 8 * r
+        total = along_z(2, z, row, *centre(2, z, row), [tend[c, z, 8 * r : 8 * r + 8, :] for c in range(5)])
+        for c in range(5):
+            tend[c, z, 8 * r : 8 * r + 8, :] = total[c]
+
+    end_planes(with_planes)
     receive_sides(2, halos[2])
-    middle_planes(section_three)
-    receive_planes(2, halos[2])
-    end_planes(section_three)
+    all_planes(section_three)
     fluid_store = pltpu.make_async_copy(fluid, fluid_out, store_sem.at[0])
     fluid_store.start()
 

time: 40.2 us -> 39.2 us (0.975)
  Pallas kernels: 36.5 us -> 35.5 us
    pallas_call x1, Pallas kernels: 36.5 us -> 35.5 us  [shards(): pl.pallas_call(kernel, out_shape=(jax.ShapeDtypeStruct((5, PZ, PX, PY), f...]
where the time goes in v5:
time: 39.2 us; the launch traced here: 39.1 us
  Pallas kernels  35.5 us (91%)
  local copies, waits for them, and re-layouts  2.91 us (7%)
  between operations  0.65 us (2%)
    pallas_call x1, Pallas kernels, shards(): pl.pallas_call(kernel, out_shape=(jax.ShapeDtypeStruct((5, PZ, PX, PY), f...  35.5 us
    unnamed x4, local copies, waits for them, and re-layouts  2.91 us

profile of v5, /device:TPU:1, one launch (start us, length us, event | category | flops | bytes accessed | tf_op | source)
XLA Modules:
  0.0 39.1 jit_solution(9627969989458478218)
XLA Ops:
  0.6 35.5 %shard_map.68 = (f32[5,8,48,128]{3,2,1,0:T(8,128)}, f32[3,48,128]{2,1,0:T(8,128)}) custom-call(f32[8,48,128]{2,1,0:T(8,128)} %density_in.1, f32[3,8,48,128]{3,2,1,0:T(8,128)} %velocity_in.1, f32[8,48,128]{2,1,0:T(8,128)} %pressure_in.1, f32[4,256]{1,0:T(4,128)} %palette_in.1, s32[8,256]{1,0:T(8,128)} %index_in.1), custom_call_target="tpu_custom_call" | custom-call | tf_op jit(solution)/shard_map/pallas_call | solution.py:670
  36.2 0.0 copy-start
  36.2 2.3 %copy.9 = f32[5,8,48,128]{3,2,1,0:T(8,128)} copy(f32[5,8,48,128]{3,2,1,0:T(8,128)} %get-tuple-element.8) | data formatting | bytes 1966080
  38.4 0.0 copy-done
  38.4 0.6 %copy.10 = f32[1,3,48,128]{3,2,1,0:T(8,128)} copy(f32[1,3,48,128]{3,2,1,0:T(8,128)S(1)} %bitcast.1) | data formatting | bytes 147456
Async XLA Ops:
  36.2 2.3 %copy-start = (f32[3,48,128]{2,1,0:T(8,128)S(1)}, f32[3,48,128]{2,1,0:T(8,128)}, u32[]{:S(2)}) copy-start(f32[3,48,128]{2,1,0:T(8,128)} %get-tuple-element.5) | copy-start | bytes 221188

commit v6 on v5

--- a/solution.py
+++ b/solution.py
@@ -219,7 +219,7 @@
                 y_part[c, rows, :] = parts[c]
             return carry
 
-        lax.fori_loop(0, NB, edge, 0, unroll=2)
+        lax.fori_loop(0, NB, edge, 0, unroll=NB)
 
     def receive_planes(s, copies):
         state, derived = states[s], prims[s]
@@ -235,7 +235,7 @@
                     derived[c, z, rows, :] = values[c]
             return carry
 
-        lax.fori_loop(0, NB, plane, 0, unroll=2)
+        lax.fori_loop(0, NB, plane, 0, unroll=NB // 2)
 
     def add(total, parts):
         return parts if total is None else [t + p for t, p in zip(total, parts)]
@@ -604,7 +604,7 @@
 
     def turn(k, carry):
         mine = (k == 3) | (k == 4) | (k == 5) | (k == 7)
-        offset = jnp.where(k < 6, 1 + lax.rem(k + 1, 3), 0)
+        offset = jnp.where(k < 6, 1 + lax.rem(k, 3), 0)
         owner = lax.rem(chip + offset, 4)
         t = 2 * owner + jnp.where(mine, core, 1 - core)
         render(t)

time: 39.2 us -> 38.2 us (0.974); the launches traced: 39.1 us -> 37.7 us
  Pallas kernels: 35.5 us -> 34.1 us
    pallas_call x1, Pallas kernels: 35.5 us -> 34.1 us  [shards(): pl.pallas_call(kernel, out_shape=(jax.ShapeDtypeStruct((5, PZ, PX, PY), f...]
where the time goes in v6:
time: 38.2 us; the launch traced here: 37.7 us
  Pallas kernels  34.1 us (89%)
  local copies, waits for them, and re-layouts  2.91 us (8%)
  between operations  0.65 us (2%)
    pallas_call x1, Pallas kernels, shards(): pl.pallas_call(kernel, out_shape=(jax.ShapeDtypeStruct((5, PZ, PX, PY), f...  34.1 us
    unnamed x4, local copies, waits for them, and re-layouts  2.91 us

profile of v6, /device:TPU:1, one launch (start us, length us, event | category | flops | bytes accessed | tf_op | source)
XLA Modules:
  0.0 37.7 jit_solution(9742699809117429709)
XLA Ops:
  0.6 34.1 %shard_map.68 = (f32[5,8,48,128]{3,2,1,0:T(8,128)}, f32[3,48,128]{2,1,0:T(8,128)}) custom-call(f32[8,48,128]{2,1,0:T(8,128)} %density_in.1, f32[3,8,48,128]{3,2,1,0:T(8,128)} %velocity_in.1, f32[8,48,128]{2,1,0:T(8,128)} %pressure_in.1, f32[4,256]{1,0:T(4,128)} %palette_in.1, s32[8,256]{1,0:T(8,128)} %index_in.1), custom_call_target="tpu_custom_call" | custom-call | tf_op jit(solution)/shard_map/pallas_call | solution.py:670
  34.7 0.0 copy-start
  34.8 2.3 %copy.9 = f32[5,8,48,128]{3,2,1,0:T(8,128)} copy(f32[5,8,48,128]{3,2,1,0:T(8,128)} %get-tuple-element.8) | data formatting | bytes 1966080
  37.0 0.0 copy-done
  37.0 0.6 %copy.10 = f32[1,3,48,128]{3,2,1,0:T(8,128)} copy(f32[1,3,48,128]{3,2,1,0:T(8,128)S(1)} %bitcast.1) | data formatting | bytes 147456
Async XLA Ops:
  34.7 2.3 %copy-start = (f32[3,48,128]{2,1,0:T(8,128)S(1)}, f32[3,48,128]{2,1,0:T(8,128)}, u32[]{:S(2)}) copy-start(f32[3,48,128]{2,1,0:T(8,128)} %get-tuple-element.5) | copy-start | bytes 221188

commit v7 on v6

--- a/solution.py
+++ b/solution.py
@@ -331,7 +331,7 @@
                 visit((PZ - 1) * k, r, True)
             return carry
 
-        lax.fori_loop(0, 2, one, 0)
+        lax.fori_loop(0, 2, one, 0, unroll=2)
 
     def inside(s):
         def visit(z, r, at_end):

time: 38.2 us -> 38 us (level)
  no operation moved by 1% of the time
where the time goes in v7:
time: 38 us; the launch traced here: 37.5 us
  Pallas kernels  34 us (89%)
  local copies, waits for them, and re-layouts  2.91 us (8%)
  between operations  0.65 us (2%)
    pallas_call x1, Pallas kernels, shards(): pl.pallas_call(kernel, out_shape=(jax.ShapeDtypeStruct((5, PZ, PX, PY), f...  34 us
    unnamed x4, local copies, waits for them, and re-layouts  2.91 us

profile of v7, /device:TPU:1, one launch (start us, length us, event | category | flops | bytes accessed | tf_op | source)
XLA Modules:
  0.0 37.5 jit_solution(18352200465161279615)
XLA Ops:
  0.6 34.0 %shard_map.68 = (f32[5,8,48,128]{3,2,1,0:T(8,128)}, f32[3,48,128]{2,1,0:T(8,128)}) custom-call(f32[8,48,128]{2,1,0:T(8,128)} %density_in.1, f32[3,8,48,128]{3,2,1,0:T(8,128)} %velocity_in.1, f32[8,48,128]{2,1,0:T(8,128)} %pressure_in.1, f32[4,256]{1,0:T(4,128)} %palette_in.1, s32[8,256]{1,0:T(8,128)} %index_in.1), custom_call_target="tpu_custom_call" | custom-call | tf_op jit(solution)/shard_map/pallas_call | solution.py:670
  34.6 0.0 copy-start
  34.6 2.3 %copy.9 = f32[5,8,48,128]{3,2,1,0:T(8,128)} copy(f32[5,8,48,128]{3,2,1,0:T(8,128)} %get-tuple-element.8) | data formatting | bytes 1966080
  36.9 0.0 copy-done
  36.9 0.6 %copy.10 = f32[1,3,48,128]{3,2,1,0:T(8,128)} copy(f32[1,3,48,128]{3,2,1,0:T(8,128)S(1)} %bitcast.1) | data formatting | bytes 147456
Async XLA Ops:
  34.6 2.3 %copy-start = (f32[3,48,128]{2,1,0:T(8,128)S(1)}, f32[3,48,128]{2,1,0:T(8,128)}, u32[]{:S(2)}) copy-start(f32[3,48,128]{2,1,0:T(8,128)} %get-tuple-element.5) | copy-start | bytes 221188

commit v8 on v7

--- a/solution.py
+++ b/solution.py
@@ -323,7 +323,7 @@
                 visit(z, r, False)
             return carry
 
-        lax.fori_loop(0, PZ, one, 0, unroll=2)
+        lax.fori_loop(0, PZ, one, 0, unroll=4)
 
     def end_planes(visit):
         def one(k, carry):

time: 38 us -> 37.9 us (level)
  no operation moved by 1% of the time
where the time goes in v8:
time: 37.9 us; the launch traced here: 37.4 us
  Pallas kernels  33.8 us (89%)
  local copies, waits for them, and re-layouts  2.91 us (8%)
  between operations  0.65 us (2%)
    pallas_call x1, Pallas kernels, shards(): pl.pallas_call(kernel, out_shape=(jax.ShapeDtypeStruct((5, PZ, PX, PY), f...  33.8 us
    unnamed x4, local copies, waits for them, and re-layouts  2.91 us

profile of v8, /device:TPU:1, one launch (start us, length us, event | category | flops | bytes accessed | tf_op | source)
XLA Modules:
  0.0 37.4 jit_solution(14525994450256074610)
XLA Ops:
  0.6 33.8 %shard_map.68 = (f32[5,8,48,128]{3,2,1,0:T(8,128)}, f32[3,48,128]{2,1,0:T(8,128)}) custom-call(f32[8,48,128]{2,1,0:T(8,128)} %density_in.1, f32[3,8,48,128]{3,2,1,0:T(8,128)} %velocity_in.1, f32[8,48,128]{2,1,0:T(8,128)} %pressure_in.1, f32[4,256]{1,0:T(4,128)} %palette_in.1, s32[8,256]{1,0:T(8,128)} %index_in.1), custom_call_target="tpu_custom_call" | custom-call | tf_op jit(solution)/shard_map/pallas_call | solution.py:670
  34.5 0.0 copy-start
  34.5 2.3 %copy.9 = f32[5,8,48,128]{3,2,1,0:T(8,128)} copy(f32[5,8,48,128]{3,2,1,0:T(8,128)} %get-tuple-element.8) | data formatting | bytes 1966080
  36.7 0.0 copy-done
  36.8 0.6 %copy.10 = f32[1,3,48,128]{3,2,1,0:T(8,128)} copy(f32[1,3,48,128]{3,2,1,0:T(8,128)S(1)} %bitcast.1) | data formatting | bytes 147456
Async XLA Ops:
  34.5 2.3 %copy-start = (f32[3,48,128]{2,1,0:T(8,128)S(1)}, f32[3,48,128]{2,1,0:T(8,128)}, u32[]{:S(2)}) copy-start(f32[3,48,128]{2,1,0:T(8,128)} %get-tuple-element.5) | copy-start | bytes 221188
